TPU v7x, 32 devices: a whole 2x2x4 slice. The times are simulated.
32 devices in a mesh: fsdp: 4 (over y, x), ctx: 8 (over z, core).
Axes of the slice: x: 2, y: 2, z: 4, core: 2. Of those that a mesh axis runs over, the one named last changes fastest.
Arguments:
- tokens: bfloat16 [12288, 768], P(('fsdp', 'ctx')), may hold values from -6 to 6
- cotangent: bfloat16 [12288, 768], P(('fsdp', 'ctx')), may hold values from -6 to 6
- w_qkv: bfloat16 [768, 2304], P('fsdp'), may hold values from -0.21875 to 0.21875
- b_query: bfloat16 [768], P('fsdp'), may hold values from -1.75 to 1.75
- b_value: bfloat16 [768], P('fsdp'), may hold values from -1.75 to 1.75
- w_out: bfloat16 [768, 768], P('fsdp'), may hold values from -3.5 to 3.5
- b_out: bfloat16 [768], P('fsdp'), may hold values from -1.75 to 1.75
- w_fc: bfloat16 [768, 3072], P('fsdp'), may hold values from -0.21875 to 0.21875
- b_fc: bfloat16 [3072], P('fsdp'), may hold values from -1.75 to 1.75
- w_proj: bfloat16 [3072, 768], P('fsdp'), may hold values from -0.109375 to 0.109375
- b_proj: bfloat16 [768], P('fsdp'), may hold values from -1.75 to 1.75
- gain1: bfloat16 [768], P('fsdp'), may hold values from 0.5 to 1.5
- shift1: bfloat16 [768], P('fsdp'), may hold values from -1.75 to 1.75
- gain2: bfloat16 [768], P('fsdp'), may hold values from 0.5 to 1.5
- shift2: bfloat16 [768], P('fsdp'), may hold values from -1.75 to 1.75
- counts: int32 [4, 8], P('fsdp'), may hold values from 192 to 384, as said below
- seq_lengths: int32 [4, 3], P('fsdp'), may hold values from 1 to 3070, as said below
Outputs:
- block_out: bfloat16 [12288, 768], P(('fsdp', 'ctx'))
- d_tokens: float32 [12288, 768], P(('fsdp', 'ctx'))
- d_w_qkv: float32 [768, 2304], P('fsdp')
- d_b_query: float32 [768], P('fsdp')
- d_b_value: float32 [768], P('fsdp')
- d_w_out: float32 [768, 768], P('fsdp')
- d_b_out: float32 [768], P('fsdp')
- d_w_fc: float32 [768, 3072], P('fsdp')
- d_b_fc: float32 [3072], P('fsdp')
- d_w_proj: float32 [3072, 768], P('fsdp')
- d_b_proj: float32 [768], P('fsdp')
- d_gain1: float32 [768], P('fsdp')
- d_shift1: float32 [768], P('fsdp')
- d_gain2: float32 [768], P('fsdp')
- d_shift2: float32 [768], P('fsdp')
Inputs may be any that keep to these rules, and one draw needn't show every extreme that they name: `counts`: each device holds between 192 and 384 live slots, its first ones; in every group some device holds exactly 384. `seq_lengths`: the lengths of a group sum to its live slots; in every group one sequence, at a position that varies, holds a slot of the first device and of the last device of the group; the other two have fewer than 96 tokens each.
All inputs are finite; a program needn't handle non-finite values.
Results may differ from a plain program's by a relative error of at most 0.018.
Values may be sent and summed in bfloat16 or wider, within the bound.
No kernel may reach another device: no remote copies, remote signals or barrier semaphores. Data moves between devices by JAX's collectives and lax.ppermute only.
A program may use at most 192 MiB of HBM per device.

v0:
```python
import jax
import jax.numpy as jnp
from jax import lax
from jax.sharding import PartitionSpec as P

HEADS = 12


EPS = 1e-05


def layer_norm(values, gain_row, shift_row):
    centre = values - jnp.mean(values, axis=1, keepdims=True)
    inverse = lax.rsqrt(jnp.mean(centre * centre, axis=1, keepdims=True) + EPS)
    normed = centre * inverse
    return (normed * gain_row + shift_row, normed, inverse)


def norm_back(grad_in, normed, inverse, gain_row):
    scaled = grad_in * gain_row
    inner_grad = inverse * (
        scaled
        - jnp.mean(scaled, axis=1, keepdims=True)
        - normed * jnp.mean(scaled * normed, axis=1, keepdims=True)
    )
    return (inner_grad, jnp.sum(grad_in * normed, axis=0), jnp.sum(grad_in, axis=0))


def contract_rows(left_side, right_side):
    return lax.dot_general(
        left_side, right_side, (((0,), (0,)), ((), ())), preferred_element_type=jnp.float32
    )


def times_transpose(left_side, right_side):
    return lax.dot_general(
        left_side, right_side, (((1,), (1,)), ((), ())), preferred_element_type=jnp.float32
    )


def gelu_tanh(values):
    return jax.nn.gelu(values, approximate=True)


def describe(slot_ids, row_count, count_row, offsets, seq_ends):
    peer_count = count_row.shape[0]
    device = slot_ids // row_count
    within = slot_ids - device * row_count
    matches = device[:, None] == jnp.arange(peer_count, dtype=jnp.int32)[None, :]
    live_count = jnp.sum(jnp.where(matches, count_row[None, :], 0), axis=1)
    first_place = jnp.sum(jnp.where(matches, offsets[None, :], 0), axis=1)
    places = first_place + within
    segment = jnp.sum((places[:, None] >= seq_ends[None, :]).astype(jnp.int32), axis=1)
    return (within < live_count, places, segment, slot_ids)


def allowed(query_info, key_info):
    q_live, q_place, q_seg, q_slot = query_info
    k_live, k_place, k_seg, k_slot = key_info
    same_seq = (
        q_live[:, None]
        & k_live[None, :]
        & (q_seg[:, None] == k_seg[None, :])
        & (k_place[None, :] <= q_place[:, None])
    )
    return same_seq | (q_slot[:, None] == k_slot[None, :])


def over_blocks(step_fn, status, pieces, row_count):
    total_rows = pieces[0].shape[0]
    block_total = total_rows // row_count
    stacked = tuple((piece.reshape((block_total, row_count) + piece.shape[1:]) for piece in pieces))

    def scan_body(state_now, scan_item):
        block_index, block_parts = scan_item
        return (step_fn(state_now, block_parts, block_index * row_count), None)

    status, unused = lax.scan(
        scan_body, status, (jnp.arange(block_total, dtype=jnp.int32), stacked)
    )
    return status


def score_grads(
    query_heads, key_heads, value_heads, grad_heads, lse_rows, delta_rows, permitted, scaling
):
    scores = (
        jnp.einsum("qhd,khd->hqk", query_heads, key_heads, preferred_element_type=jnp.float32)
        * scaling
    )
    probabilities = jnp.where(permitted[None], jnp.exp(scores - lse_rows[:, :, None]), 0.0)
    grad_probs = jnp.einsum(
        "qhd,khd->hqk", grad_heads, value_heads, preferred_element_type=jnp.float32
    )
    grad_scores = (probabilities * (grad_probs - delta_rows[:, :, None])).astype(jnp.bfloat16)
    return (probabilities.astype(jnp.bfloat16), grad_scores)


def body(
    tokens,
    cotangent,
    w_qkv,
    b_query,
    b_value,
    w_out,
    b_out,
    w_fc,
    b_fc,
    w_proj,
    b_proj,
    gain1,
    shift1,
    gain2,
    shift2,
    counts,
    seq_lengths,
):
    row_count, feature_count = tokens.shape
    peer_count = lax.axis_size("ctx")
    my_index = lax.axis_index("ctx")
    head_count = HEADS
    head_width = feature_count // head_count
    scaling = head_width ** (-0.5)
    count_row = counts[0]
    offsets = jnp.cumsum(count_row) - count_row
    seq_ends = jnp.cumsum(seq_lengths[0])

    def locate(first_slot, length):
        return describe(
            first_slot + jnp.arange(length, dtype=jnp.int32),
            row_count,
            count_row,
            offsets,
            seq_ends,
        )

    own_rows = locate(my_index * row_count, row_count)
    fp32 = jnp.float32
    bf16 = jnp.bfloat16
    (
        qkv_full,
        query_bias,
        value_bias,
        out_full,
        out_bias,
        fc_full,
        fc_bias,
        proj_full,
        proj_bias,
        gain_one,
        shift_one,
        gain_two,
        shift_two,
    ) = (
        lax.all_gather(w_qkv, "fsdp", axis=0, tiled=True),
        lax.all_gather(b_query, "fsdp", axis=0, tiled=True),
        lax.all_gather(b_value, "fsdp", axis=0, tiled=True),
        lax.all_gather(w_out, "fsdp", axis=0, tiled=True),
        lax.all_gather(b_out, "fsdp", axis=0, tiled=True),
        lax.all_gather(w_fc, "fsdp", axis=0, tiled=True),
        lax.all_gather(b_fc, "fsdp", axis=0, tiled=True),
        lax.all_gather(w_proj, "fsdp", axis=0, tiled=True),
        lax.all_gather(b_proj, "fsdp", axis=0, tiled=True),
        lax.all_gather(gain1, "fsdp", axis=0, tiled=True),
        lax.all_gather(shift1, "fsdp", axis=0, tiled=True),
        lax.all_gather(gain2, "fsdp", axis=0, tiled=True),
        lax.all_gather(shift2, "fsdp", axis=0, tiled=True),
    )
    inputs = tokens.astype(fp32)
    normed_one, unit_one, inverse_one = layer_norm(
        inputs, gain_one.astype(fp32), shift_one.astype(fp32)
    )
    normed_low = normed_one.astype(bf16)
    bias_row = jnp.concatenate([query_bias, jnp.zeros_like(query_bias), value_bias]).astype(fp32)
    packed = (jnp.dot(normed_low, qkv_full, preferred_element_type=fp32) + bias_row).astype(bf16)
    query_rows = packed[:, :feature_count]
    key_rows = packed[:, feature_count : 2 * feature_count]
    value_rows = packed[:, 2 * feature_count :]
    query_heads = query_rows.reshape(row_count, head_count, head_width)

    def forward_step(status, pieces, first_row):
        running_max, running_sum, running_acc = status
        key_piece, value_piece = pieces
        length = key_piece.shape[0]
        key_heads = key_piece.reshape(length, head_count, head_width)
        value_heads = value_piece.reshape(length, head_count, head_width)
        scores = (
            jnp.einsum("qhd,khd->hqk", query_heads, key_heads, preferred_element_type=fp32)
            * scaling
        )
        permitted = allowed(own_rows, locate(first_row, length))
        scores = jnp.where(permitted[None], scores, -jnp.inf)
        new_max = jnp.maximum(running_max, jnp.max(scores, axis=2))
        fading = jnp.exp(running_max - new_max)
        weights = jnp.exp(scores - new_max[:, :, None])
        running_sum = running_sum * fading + jnp.sum(weights, axis=2)
        update = jnp.einsum(
            "hqk,khd->qhd", weights.astype(bf16), value_heads, preferred_element_type=fp32
        )
        running_acc = running_acc * jnp.transpose(fading)[:, :, None] + update
        return (new_max, running_sum, running_acc)

    start_state = (
        jnp.full((head_count, row_count), -1e30, fp32),
        jnp.zeros((head_count, row_count), fp32),
        jnp.zeros((row_count, head_count, head_width), fp32),
    )
    final_max, final_sum, final_acc = over_blocks(
        forward_step,
        start_state,
        (
            lax.all_gather(key_rows, "ctx", axis=0, tiled=True),
            lax.all_gather(value_rows, "ctx", axis=0, tiled=True),
        ),
        row_count,
    )
    attended_heads = final_acc / jnp.transpose(final_sum)[:, :, None]
    attended = attended_heads.reshape(row_count, feature_count)
    log_total = final_max + jnp.log(final_sum)
    attended_low = attended.astype(bf16)
    middle = (
        inputs
        + jnp.dot(attended_low, out_full, preferred_element_type=fp32)
        + out_bias.astype(fp32)
    )
    normed_two, unit_two, inverse_two = layer_norm(
        middle, gain_two.astype(fp32), shift_two.astype(fp32)
    )
    normed_two_low = normed_two.astype(bf16)
    hidden = jnp.dot(normed_two_low, fc_full, preferred_element_type=fp32) + fc_bias.astype(fp32)
    activated = gelu_tanh(hidden).astype(bf16)
    output = (
        middle + jnp.dot(activated, proj_full, preferred_element_type=fp32) + proj_bias.astype(fp32)
    )
    output_low = output.astype(bf16)
    qkv_full, out_full, fc_full, proj_full, gain_one, gain_two = (
        lax.all_gather(w_qkv, "fsdp", axis=0, tiled=True),
        lax.all_gather(w_out, "fsdp", axis=0, tiled=True),
        lax.all_gather(w_fc, "fsdp", axis=0, tiled=True),
        lax.all_gather(w_proj, "fsdp", axis=0, tiled=True),
        lax.all_gather(gain1, "fsdp", axis=0, tiled=True),
        lax.all_gather(gain2, "fsdp", axis=0, tiled=True),
    )
    live_rows = own_rows[0].astype(fp32)[:, None]
    grad_out = cotangent.astype(fp32) * live_rows
    grad_out_low = grad_out.astype(bf16)
    grad_proj = contract_rows(activated, grad_out_low)
    grad_proj_bias = jnp.sum(grad_out, axis=0)
    grad_act = times_transpose(grad_out_low, proj_full)
    grad_hidden = jax.vjp(gelu_tanh, hidden)[1](grad_act)[0]
    grad_hidden_low = grad_hidden.astype(bf16)
    grad_fc = contract_rows(normed_two_low, grad_hidden_low)
    grad_fc_bias = jnp.sum(grad_hidden_low.astype(fp32), axis=0)
    grad_normed_two = times_transpose(grad_hidden_low, fc_full)
    grad_mid_norm, grad_gain_two, grad_shift_two = norm_back(
        grad_normed_two, unit_two, inverse_two, gain_two.astype(fp32)
    )
    grad_middle = grad_out + grad_mid_norm
    grad_middle_low = grad_middle.astype(bf16)
    grad_out_proj = contract_rows(attended_low, grad_middle_low)
    grad_out_bias = jnp.sum(grad_middle_low.astype(fp32), axis=0)
    grad_attended = times_transpose(grad_middle_low, out_full).astype(bf16)
    grad_heads = grad_attended.reshape(row_count, head_count, head_width)
    delta_rows = jnp.transpose(jnp.sum(grad_heads.astype(fp32) * attended_heads, axis=2))

    def back_step(status, pieces, first_row):
        grad_query, grad_keys = status
        key_piece, value_piece = pieces
        length = key_piece.shape[0]
        key_heads = key_piece.reshape(length, head_count, head_width)
        value_heads = value_piece.reshape(length, head_count, head_width)
        permitted = allowed(own_rows, locate(first_row, length))
        probs_low, grad_scores = score_grads(
            query_heads,
            key_heads,
            value_heads,
            grad_heads,
            log_total,
            delta_rows,
            permitted,
            scaling,
        )
        grad_query = (
            grad_query
            + jnp.einsum("hqk,khd->qhd", grad_scores, key_heads, preferred_element_type=fp32)
            * scaling
        )
        grad_key_part = (
            jnp.einsum("hqk,qhd->khd", grad_scores, query_heads, preferred_element_type=fp32)
            * scaling
        )
        grad_value_part = jnp.einsum(
            "hqk,qhd->khd", probs_low, grad_heads, preferred_element_type=fp32
        )
        joined = jnp.concatenate(
            [
                grad_key_part.reshape(length, feature_count),
                grad_value_part.reshape(length, feature_count),
            ],
            axis=1,
        )
        current = lax.dynamic_slice_in_dim(grad_keys, first_row, length, 0)
        grad_keys = lax.dynamic_update_slice_in_dim(grad_keys, current + joined, first_row, 0)
        return (grad_query, grad_keys)

    keys_start = jnp.zeros((peer_count * row_count, 2 * feature_count), fp32)
    grad_query, grad_keys = over_blocks(
        back_step,
        (jnp.zeros((row_count, head_count, head_width), fp32), keys_start),
        (
            lax.all_gather(key_rows, "ctx", axis=0, tiled=True),
            lax.all_gather(value_rows, "ctx", axis=0, tiled=True),
        ),
        row_count,
    )
    grad_kv = lax.psum_scatter(
        grad_keys.astype(jnp.bfloat16), "ctx", scatter_dimension=0, tiled=True
    ).astype(jnp.float32)
    grad_packed = jnp.concatenate(
        [grad_query.reshape(row_count, feature_count), grad_kv], axis=1
    ).astype(bf16)
    grad_packed_wide = grad_packed.astype(fp32)
    grad_query_bias = jnp.sum(grad_packed_wide[:, :feature_count], axis=0)
    grad_value_bias = jnp.sum(grad_packed_wide[:, 2 * feature_count :], axis=0)
    grad_qkv = contract_rows(normed_low, grad_packed)
    grad_normed_one = times_transpose(grad_packed, qkv_full)
    grad_in_norm, grad_gain_one, grad_shift_one = norm_back(
        grad_normed_one, unit_one, inverse_one, gain_one.astype(fp32)
    )
    grad_tokens = grad_middle + grad_in_norm
    (
        sum_qkv,
        sum_qbias,
        sum_vbias,
        sum_out,
        sum_obias,
        sum_fc,
        sum_fbias,
        sum_proj,
        sum_pbias,
        sum_gain_one,
        sum_shift_one,
        sum_gain_two,
        sum_shift_two,
    ) = (
        lax.psum_scatter(
            grad_qkv.astype(jnp.bfloat16), "fsdp", scatter_dimension=0, tiled=True
        ).astype(jnp.float32),
        lax.psum_scatter(
            grad_query_bias.astype(jnp.bfloat16), "fsdp", scatter_dimension=0, tiled=True
        ).astype(jnp.float32),
        lax.psum_scatter(
            grad_value_bias.astype(jnp.bfloat16), "fsdp", scatter_dimension=0, tiled=True
        ).astype(jnp.float32),
        lax.psum_scatter(
            grad_out_proj.astype(jnp.bfloat16), "fsdp", scatter_dimension=0, tiled=True
        ).astype(jnp.float32),
        lax.psum_scatter(
            grad_out_bias.astype(jnp.bfloat16), "fsdp", scatter_dimension=0, tiled=True
        ).astype(jnp.float32),
        lax.psum_scatter(
            grad_fc.astype(jnp.bfloat16), "fsdp", scatter_dimension=0, tiled=True
        ).astype(jnp.float32),
        lax.psum_scatter(
            grad_fc_bias.astype(jnp.bfloat16), "fsdp", scatter_dimension=0, tiled=True
        ).astype(jnp.float32),
        lax.psum_scatter(
            grad_proj.astype(jnp.bfloat16), "fsdp", scatter_dimension=0, tiled=True
        ).astype(jnp.float32),
        lax.psum_scatter(
            grad_proj_bias.astype(jnp.bfloat16), "fsdp", scatter_dimension=0, tiled=True
        ).astype(jnp.float32),
        lax.psum_scatter(
            grad_gain_one.astype(jnp.bfloat16), "fsdp", scatter_dimension=0, tiled=True
        ).astype(jnp.float32),
        lax.psum_scatter(
            grad_shift_one.astype(jnp.bfloat16), "fsdp", scatter_dimension=0, tiled=True
        ).astype(jnp.float32),
        lax.psum_scatter(
            grad_gain_two.astype(jnp.bfloat16), "fsdp", scatter_dimension=0, tiled=True
        ).astype(jnp.float32),
        lax.psum_scatter(
            grad_shift_two.astype(jnp.bfloat16), "fsdp", scatter_dimension=0, tiled=True
        ).astype(jnp.float32),
    )
    totals = (
        lax.psum(sum_qkv.astype(jnp.bfloat16), "ctx").astype(jnp.float32),
        lax.psum(sum_qbias.astype(jnp.bfloat16), "ctx").astype(jnp.float32),
        lax.psum(sum_vbias.astype(jnp.bfloat16), "ctx").astype(jnp.float32),
        lax.psum(sum_out.astype(jnp.bfloat16), "ctx").astype(jnp.float32),
        lax.psum(sum_obias.astype(jnp.bfloat16), "ctx").astype(jnp.float32),
        lax.psum(sum_fc.astype(jnp.bfloat16), "ctx").astype(jnp.float32),
        lax.psum(sum_fbias.astype(jnp.bfloat16), "ctx").astype(jnp.float32),
        lax.psum(sum_proj.astype(jnp.bfloat16), "ctx").astype(jnp.float32),
        lax.psum(sum_pbias.astype(jnp.bfloat16), "ctx").astype(jnp.float32),
        lax.psum(sum_gain_one.astype(jnp.bfloat16), "ctx").astype(jnp.float32),
        lax.psum(sum_shift_one.astype(jnp.bfloat16), "ctx").astype(jnp.float32),
        lax.psum(sum_gain_two.astype(jnp.bfloat16), "ctx").astype(jnp.float32),
        lax.psum(sum_shift_two.astype(jnp.bfloat16), "ctx").astype(jnp.float32),
    )
    return (
        output_low,
        grad_tokens,
        totals[0],
        totals[1],
        totals[2],
        totals[3],
        totals[4],
        totals[5],
        totals[6],
        totals[7],
        totals[8],
        totals[9],
        totals[10],
        totals[11],
        totals[12],
    )


def solution(mesh):
    in_specs = (
        P(("fsdp", "ctx"), None),
        P(("fsdp", "ctx"), None),
        P("fsdp", None),
        P("fsdp"),
        P("fsdp"),
        P("fsdp", None),
        P("fsdp"),
        P("fsdp", None),
        P("fsdp"),
        P("fsdp", None),
        P("fsdp"),
        P("fsdp"),
        P("fsdp"),
        P("fsdp"),
        P("fsdp"),
        P("fsdp", None),
        P("fsdp", None),
    )
    out_specs = (
        P(("fsdp", "ctx"), None),
        P(("fsdp", "ctx"), None),
        P("fsdp", None),
        P("fsdp"),
        P("fsdp"),
        P("fsdp", None),
        P("fsdp"),
        P("fsdp", None),
        P("fsdp"),
        P("fsdp", None),
        P("fsdp"),
        P("fsdp"),
        P("fsdp"),
        P("fsdp"),
        P("fsdp"),
    )
    return jax.shard_map(body, mesh=mesh, in_specs=in_specs, out_specs=out_specs, check_vma=False)
```

profile of v0, /device:TPU:0, one launch (start us, length us, event | category | flops | bytes accessed | tf_op | source)
XLA Modules:
  0.0 900.8 jit_solution(15853551755257665816)
XLA Ops:
  15.8 17.8 %all-reduce.20 = (bf16[768]{0:T(1024)(128)(2,1)S(1)}, bf16[768]{0:T(1024)(128)(2,1)S(1)}, bf16[768]{0:T(1024)(128)(2,1)S(1)}, bf16[768]{0:T(1024)(128)(2,1)S(1)}...) all-reduce(bf16[768]{0:T(1024)(128)(2,1)S(1)} %dynamic-update-slice, ...), channel_id=1, replica_groups=mesh['fsdp'=4,'ctx'=8] {'fsdp'}, use_global_device_ids=true, to_apply=%add.3 | all-reduce | flops 5376 | bytes 21504
  35.3 24.7 %all-gather.8.cloned.1.call-done = bf16[768,2304]{1,0:T(8,128)(2,1)} async-done(((bf16[192,2304]{1,0:T(8,128)(2,1)}), bf16[768,2304]{1,0:T(8,128)(2,1)}) %all-gather.8.cloned.1.call-update) | async-done | bytes 3538960 | tf_op jit(solution)/shard_map/all_gather | solution.py:155
  60.0 3.7 fusion.43
  71.0 8.3 all-gather
  81.3 35.5 %all-gather.12.cloned.1.call-done = bf16[3072,768]{1,0:T(8,128)(2,1)} async-done(((bf16[384,768]{1,0:T(8,128)(2,1)}), bf16[3072,768]{1,0:T(8,128)(2,1)}) %all-gather.12.cloned.1.call-update) | async-done | bytes 4718608 | tf_op jit(solution)/shard_map/all_gather | solution.py:213
  116.9 6.7 copy.70
  123.6 46.1 %all-gather.10.cloned.1.call-done = bf16[3072,768]{1,0:T(8,128)(2,1)} async-done(((bf16[384,768]{1,0:T(8,128)(2,1)}), bf16[3072,768]{1,0:T(8,128)(2,1)}) %all-gather.10.cloned.1.call-update) | async-done | bytes 4718608 | tf_op jit(solution)/shard_map/all_gather | solution.py:212
  169.6 6.7 copy.69
  176.8 85.6 %while.32 = (s32[]{:T(128)}, f32[12,384]{1,0:T(8,128)}, f32[12,384]{1,0:T(8,128)}, f32[384,12,64]{0,2,1:T(8,128)S(1)}, pred[384]{0:T(512)(128)(4,1)S(1)}, /*inde...) while((s32[]{:T(128)}, f32[12,384]{1,0:T(8,128)}, ...), condition=%wide.region_13.14_spmd.clone, body=%wide.region_7.13_spmd.clone.sunk | while | flops 474424320 | bytes 28855300 | solution.py:78
  184.7 2.2 fusion.150
  195.4 2.2 fusion.150
  206.1 2.2 fusion.150
  216.8 2.2 fusion.150
  227.5 2.2 fusion.150
  238.2 2.2 fusion.150
  248.9 2.2 fusion.150
  259.6 2.2 fusion.150
  264.1 2.4 fusion.85
  268.4 7.0 convolution_add_fusion.1
  275.5 40.1 %all-gather.18.cloned.1.call-done = bf16[3072,768]{1,0:T(8,128)(2,1)} async-done(((bf16[768,768]{1,0:T(8,128)(2,1)}), bf16[3072,768]{1,0:T(8,128)(2,1)}) %all-gather.18.cloned.1.call-update) | async-done | bytes 4718608 | tf_op jit(solution)/shard_map/all_gather | solution.py:162
  315.6 9.0 fusion.86
  324.6 2.9 multiply_reduce_fusion
  327.5 1.9 convert_reduce_fusion.4
  330.9 2.1 copy.71
  333.0 2.2 multiply_reduce_fusion.1
  335.8 8.9 broadcast_in_dim.186
  344.6 128.1 %while.33 = (s32[]{:T(128)}, f32[384,12,64]{0,2,1:T(8,128)S(1)}, f32[3072,1536]{0,1:T(8,128)}, bf16[8,384,768]{1,2,0:T(8,128)(2,1)}, pred[384]{0:T(512)(128)(4,1...) while((s32[]{:T(128)}, f32[384,12,64]{0,2,1:T(8,128)S(1)}, ...), condition=%wide.region_23.24_spmd.clone, body=%wide.region_19.23_spmd.clone.sunk | while | flops 1153579008 | bytes 53167164 | solution.py:78
  352.5 2.4 fusion.164
  357.2 3.5 fusion.167
  368.6 2.4 fusion.164
  373.2 3.5 fusion.167
  384.6 2.4 fusion.164
  389.3 3.5 fusion.167
  400.7 2.4 fusion.164
  405.4 3.4 fusion.167
  416.7 2.4 fusion.164
  421.4 3.4 fusion.167
  432.6 2.4 fusion.164
  437.3 3.4 fusion.167
  448.6 2.4 fusion.164
  453.3 3.4 fusion.167
  464.6 2.4 fusion.164
  469.3 3.4 fusion.167
  472.7 11.7 %convert_element_type.246 = bf16[3072,1536]{0,1:T(8,128)(2,1)} convert(f32[3072,1536]{0,1:T(8,128)} %get-tuple-element.418) | non-fusion elementwise | flops 4718592 | bytes 28311552 | tf_op jit(solution)/shard_map/convert_element_type | solution.py:317
  484.4 12.7 %copy.78 = bf16[3072,1536]{1,0:T(8,128)(2,1)} copy(bf16[3072,1536]{0,1:T(8,128)(2,1)} %convert_element_type.246) | data formatting | bytes 18874368
  498.2 1.8 convolution_convert_fusion.3
  500.1 7.1 convolution_convert_fusion.1
  508.2 7.4 convolution_convert_fusion
  515.8 80.9 %reduce-scatter.16.cloned.1.call-done = bf16[384,1536]{1,0:T(8,128)(2,1)} async-done(((bf16[3072,1536]{1,0:T(8,128)(2,1)}), bf16[384,1536]{1,0:T(8,128)(2,1)}) %reduce-scatter.16.cloned.1.call-update) | async-done | bytes 1179664
  596.8 1.7 copy.79
  598.5 4.8 convolution_convert_fusion.2
  608.0 2.1 fusion.63
  611.4 3.5 fusion.59
  614.8 12.4 %reduce-scatter.10.cloned.1.call-done = bf16[192,768]{1,0:T(8,128)(2,1)} async-done(((bf16[768,768]{1,0:T(8,128)(2,1)}), bf16[192,768]{1,0:T(8,128)(2,1)}) %reduce-scatter.10.cloned.1.call-update) | async-done | bytes 294928 | tf_op jit(solution)/shard_map/reduce_scatter | solution.py:355
  627.2 60.1 %reduce-scatter.12.cloned.1.call-done = bf16[192,3072]{1,0:T(8,128)(2,1)} async-done(((bf16[768,3072]{1,0:T(8,128)(2,1)}), bf16[192,3072]{1,0:T(8,128)(2,1)}) %reduce-scatter.12.cloned.1.call-update) | async-done | bytes 1179664 | tf_op jit(solution)/shard_map/reduce_scatter | solution.py:361
  687.3 60.0 %reduce-scatter.14.cloned.1.call-done = bf16[768,768]{1,0:T(8,128)(2,1)} async-done(((bf16[3072,768]{1,0:T(8,128)(2,1)}), bf16[768,768]{1,0:T(8,128)(2,1)}) %reduce-scatter.14.cloned.1.call-update) | async-done | bytes 1179664 | tf_op jit(solution)/shard_map/reduce_scatter | solution.py:367
  747.3 50.4 %reduce-scatter.8.cloned.1.call-done = bf16[192,2304]{1,0:T(8,128)(2,1)} async-done(((bf16[768,2304]{1,0:T(8,128)(2,1)}), bf16[192,2304]{1,0:T(8,128)(2,1)}) %reduce-scatter.8.cloned.1.call-update) | async-done | bytes 884752 | tf_op jit(solution)/shard_map/reduce_scatter | solution.py:346
  797.8 2.0 slice_reduce_fusion
  799.9 15.9 %all-reduce.19 = (bf16[768]{0:T(1024)(128)(2,1)S(1)}, bf16[768]{0:T(1024)(128)(2,1)S(1)}, bf16[768]{0:T(1024)(128)(2,1)S(1)}, bf16[768]{0:T(1024)(128)(2,1)S(1)}...) all-reduce(bf16[768]{0:T(1024)(128)(2,1)} %dynamic-update-slice.7, ...), channel_id=1, replica_groups=mesh['fsdp'=4,'ctx'=8] {'fsdp'}, use_global_device_ids=true, to_apply=%add.7 | all-reduce | flops 9984 | bytes 39936
  816.4 15.0 %all-reduce.17 = (bf16[192]{0:T(256)(128)(2,1)S(1)}, bf16[192]{0:T(256)(128)(2,1)S(1)}, bf16[192]{0:T(256)(128)(2,1)S(1)}, bf16[768]{0:T(1024)(128)(2,1)S(1)}, b...) all-reduce(bf16[192]{0:T(256)(128)(2,1)S(1)} %dynamic-slice.9, ...), channel_id=1, replica_groups=mesh['fsdp'=4,'ctx'=8] {'ctx'}, use_global_device_ids=true, to_apply=%region_31.32 | all-reduce | flops 2304 | bytes 9216 | tf_op jit(solution)/shard_map/psum | solution.py:388
  838.1 7.5 fusion.52
  845.6 40.5 %all-reduce.23.cloned.1.call-done = (bf16[192,2304]{1,0:T(8,128)(2,1)}, bf16[192,768]{1,0:T(8,128)(2,1)}, bf16[192,3072]{1,0:T(8,128)(2,1)}, bf16[768,768]{1,0:T(8,128)(2,1)}) async-done(((bf16[192,2304]{1,0:T(8,128)(2,1)}, bf16[192,768]{1,0:T(8,128)(2,1)}, bf16[192,3072]{1,0:T(8,128)(2,1)}, bf16[768,768]{1,0:T(8,128)(2,1)}), (bf16[192,2304]{1,0:T(8,128)(2,1)}, bf16[192,768]{1,0:T(8,128)(2,1)}, ...) | async-done | bytes 3538960 | tf_op jit(solution)/shard_map/psum | solution.py:387
  886.1 1.9 convert_element_type.255
  888.0 2.5 convert_element_type.248
  (518 shorter events, 179.7 us)
Async XLA Ops:
  7.2 27.8 %copy-start = (bf16[384,768]{1,0:T(8,128)(2,1)S(1)}, bf16[384,768]{1,0:T(8,128)(2,1)}, u32[]{:S(2)}) copy-start(bf16[384,768]{1,0:T(8,128)(2,1)} %param.21) | copy-start | bytes 1769476
  7.2 52.8 %all-gather.8.cloned.1.call-start = ((), (), s32[]{:S(2)}) async-start(), calls=%async_computation.5 | async-start | bytes 4423680 | tf_op jit(solution)/shard_map/all_gather | solution.py:155
  7.9 108.9 %all-gather.12.cloned.1.call-start = ((), (), s32[]{:S(2)}) async-start(), calls=%async_computation.7 | async-start | bytes 5308416 | tf_op jit(solution)/shard_map/all_gather | solution.py:213
  33.7 30.0 %copy-start.30 = (f32[768]{0:T(1024)}, f32[768]{0:T(1024)S(1)}, u32[]{:S(2)}) copy-start(f32[768]{0:T(1024)S(1)} %convert_element_type.224) | copy-start | bytes 9220
  33.7 30.0 %copy-start.42 = (f32[768]{0:T(1024)}, f32[768]{0:T(1024)S(1)}, u32[]{:S(2)}) copy-start(f32[768]{0:T(1024)S(1)} %convert_element_type.225) | copy-start | bytes 9220
  35.0 28.8 %copy-start.23 = (f32[384]{0:T(512)}, f32[384]{0:T(512)S(1)}, u32[]{:S(2)}) copy-start(f32[384]{0:T(512)S(1)} %broadcast_multiply_fusion.5) | copy-start | bytes 4612
  35.3 28.4 %copy-start.35 = (f32[384]{0:T(512)}, f32[384]{0:T(512)S(1)}, u32[]{:S(2)}) copy-start(f32[384]{0:T(512)S(1)} %add_rsqrt_fusion.1) | copy-start | bytes 4612
  65.0 2.6 copy-start.19
  65.0 3.3 copy-start.53
  65.0 4.2 copy-start.48
  65.0 104.6 %all-gather.10.cloned.1.call-start = ((), (), s32[]{:S(2)}) async-start(), calls=%async_computation.6 | async-start | bytes 5308416 | tf_op jit(solution)/shard_map/all_gather | solution.py:212
  65.8 198.3 %all-gather.14.cloned.1.call-start = ((), (), s32[]{:S(2)}) async-start(), calls=%async_computation.8 | async-start | bytes 1474560 | tf_op jit(solution)/shard_map/all_gather | solution.py:158
  66.3 202.1 %all-gather.16.cloned.1.call-start = ((), (), s32[]{:S(2)}) async-start(), calls=%async_computation.9 | async-start | bytes 5898240 | tf_op jit(solution)/shard_map/all_gather | solution.py:160
  66.9 248.6 %all-gather.18.cloned.1.call-start = ((), (), s32[]{:S(2)}) async-start(), calls=%async_computation.10 | async-start | bytes 5898240 | tf_op jit(solution)/shard_map/all_gather | solution.py:162
  67.5 529.3 %reduce-scatter.16.cloned.1.call-start = ((), (), s32[]{:S(2)}) async-start(), calls=%async_computation.15 | async-start | bytes 10616832
  68.5 11.5 %copy-start.20 = (s32[3,1]{0,1:T(1,128)}, s32[3,1]{0,1:T(1,128)S(1)}, u32[]{:S(2)}) copy-start(s32[3,1]{0,1:T(1,128)S(1)} %reduce-window.14) | copy-start | bytes 40
  184.7 2.2 copy-start.12
  195.4 2.2 copy-start.12
  206.1 2.2 copy-start.12
  216.8 2.2 copy-start.12
  227.5 2.2 copy-start.12
  238.2 2.2 copy-start.12
  248.9 2.2 copy-start.12
  259.6 2.2 copy-start.12
  262.4 4.1 copy-start.1
  264.1 3.7 copy-start.6
  264.1 3.7 copy-start.14
  266.5 58.0 %copy-start.28 = (f32[384]{0:T(512)}, f32[384]{0:T(512)S(1)}, u32[]{:S(2)}) copy-start(f32[384]{0:T(512)S(1)} %broadcast_multiply_fusion.4) | copy-start | bytes 4612
  267.8 56.8 %copy-start.39 = (f32[384]{0:T(512)}, f32[384]{0:T(512)S(1)}, u32[]{:S(2)}) copy-start(f32[384]{0:T(512)S(1)} %add_rsqrt_fusion) | copy-start | bytes 4612
  268.4 47.1 %copy-start.9 = (bf16[384,768]{1,0:T(8,128)(2,1)S(1)}, bf16[384,768]{1,0:T(8,128)(2,1)}, u32[]{:S(2)}) copy-start(bf16[384,768]{1,0:T(8,128)(2,1)} %param.22) | copy-start | bytes 1769476
  268.4 47.1 %copy-start.25 = (f32[384]{0:T(512)S(1)}, f32[384]{0:T(512)}, u32[]{:S(2)}) copy-start(f32[384]{0:T(512)} %get-tuple-element.769) | copy-start | bytes 4612
  315.5 9.0 %copy-start.3 = (f32[384,768]{1,0:T(8,128)S(1)}, f32[384,768]{1,0:T(8,128)}, u32[]{:S(2)}) copy-start(f32[384,768]{1,0:T(8,128)} %copy-done.2) | copy-start | bytes 3538948
  315.5 9.0 %copy-start.32 = (f32[768]{0:T(1024)S(1)}, f32[768]{0:T(1024)}, u32[]{:S(2)}) copy-start(f32[768]{0:T(1024)} %convert_element_type.232) | copy-start | bytes 9220
  315.5 9.0 %copy-start.51 = (bf16[768,3072]{1,0:T(8,128)(2,1)S(1)}, bf16[768,3072]{1,0:T(8,128)(2,1)}, u32[]{:S(2)}) copy-start(bf16[768,3072]{1,0:T(8,128)(2,1)} %all-gather.16.cloned.1.call-done) | copy-start | bytes 14155780
  324.6 2.9 copy-start.55
  324.6 2.9 copy-start.10
  324.6 2.9 copy-start.26
  327.5 1.9 copy-start.18
  497.1 2.9 copy-start.29
  497.2 2.9 copy-start.33
  497.2 2.9 copy-start.40
  497.2 2.9 copy-start.43
  497.2 130.0 %reduce-scatter.10.cloned.1.call-start = ((), (), s32[]{:S(2)}) async-start(), calls=%async_computation.12 | async-start | bytes 1474560 | tf_op jit(solution)/shard_map/reduce_scatter | solution.py:355
  500.0 187.4 %reduce-scatter.12.cloned.1.call-start = ((), (), s32[]{:S(2)}) async-start(), calls=%async_computation.13 | async-start | bytes 5898240 | tf_op jit(solution)/shard_map/reduce_scatter | solution.py:361
  507.2 240.1 %reduce-scatter.14.cloned.1.call-start = ((), (), s32[]{:S(2)}) async-start(), calls=%async_computation.14 | async-start | bytes 5898240 | tf_op jit(solution)/shard_map/reduce_scatter | solution.py:367
  515.7 282.0 %reduce-scatter.8.cloned.1.call-start = ((), (), s32[]{:S(2)}) async-start(), calls=%async_computation.11 | async-start | bytes 4423680 | tf_op jit(solution)/shard_map/reduce_scatter | solution.py:346
  515.7 82.8 %copy-start.24 = (f32[384]{0:T(512)S(1)}, f32[384]{0:T(512)}, u32[]{:S(2)}) copy-start(f32[384]{0:T(512)} %copy-done.23) | copy-start | bytes 4612
  515.7 82.8 %copy-start.31 = (f32[768]{0:T(1024)S(1)}, f32[768]{0:T(1024)}, u32[]{:S(2)}) copy-start(f32[768]{0:T(1024)} %copy-done.30) | copy-start | bytes 9220
  515.7 82.8 %copy-start.36 = (f32[384]{0:T(512)S(1)}, f32[384]{0:T(512)}, u32[]{:S(2)}) copy-start(f32[384]{0:T(512)} %copy-done.35) | copy-start | bytes 4612
  603.3 2.0 copy-start.54
  603.3 282.8 %all-reduce.23.cloned.1.call-start = ((), (), s32[]{:S(2)}) async-start(), calls=%async_computation.16 | async-start | bytes 7077888 | tf_op jit(solution)/shard_map/psum | solution.py:387
  608.0 2.1 copy-start.37
  608.0 3.4 copy-start.52
  797.7 2.1 copy-start.34
  797.7 2.1 copy-start.41
  797.7 2.1 copy-start.44
  797.7 2.1 copy-start.45
  797.8 2.1 copy-start.46
  797.8 2.1 copy-start.47
  797.8 38.8 %copy-start.50 = (f32[384]{0:T(512)S(1)}, f32[384]{0:T(512)}, u32[]{:S(2)}) copy-start(f32[384]{0:T(512)} %get-tuple-element.664) | copy-start | bytes 4612
  797.8 38.8 %copy-start.49 = (f32[384]{0:T(512)S(1)}, f32[384]{0:T(512)}, u32[]{:S(2)}) copy-start(f32[384]{0:T(512)} %get-tuple-element.665) | copy-start | bytes 4612
  797.8 38.8 %copy-start.15 = (f32[384,768]{1,0:T(8,128)S(1)}, f32[384,768]{1,0:T(8,128)}, u32[]{:S(2)}) copy-start(f32[384,768]{1,0:T(8,128)} %get-tuple-element.791) | copy-start | bytes 3538948
  797.8 38.8 %copy-start.38 = (f32[384]{0:T(512)S(1)}, f32[384]{0:T(512)}, u32[]{:S(2)}) copy-start(f32[384]{0:T(512)} %copy-done.35) | copy-start | bytes 4612
  886.1 4.4 copy-start.17
  (46 other events, 53.5 us)
Sparse Core Ops, SparseCore 0:
  9.9 50.0 all-gather.7
  65.1 51.6 all-gather.11
  119.1 50.5 all-gather.9
  171.3 26.5 all-gather.13
  199.6 57.1 all-gather.15
  258.4 57.0 all-gather.17
  497.3 99.4 reduce-scatter.15
  600.3 26.9 reduce-scatter.9
  630.2 57.0 reduce-scatter.11
  690.2 57.0 reduce-scatter.13
  750.4 47.2 reduce-scatter.7
  800.2 85.8 all-reduce.22
where the time goes:
time: 907 us; the launch traced here: 901 us
  waiting for transfers between devices  454 us (50%)
  matrix products  145 us (16%)
  other arithmetic  112 us (12%)
  local copies, waits for them, and re-layouts  104 us (11%)
  blocking collectives  57 us (6%)
  between operations  17 us (2%)
  loops' own time  12.2 us (1%)
    unnamed x13, waiting for transfers between devices  84 us
    reduce_scatter x1, waiting for transfers between devices, body(): lax.psum_scatter(grad_fc.astype(jnp.bfloat16), 'fsdp', scatter_dimension=...  60.1 us
    reduce_scatter x1, waiting for transfers between devices, body(): lax.psum_scatter(grad_proj.astype(jnp.bfloat16), 'fsdp', scatter_dimensio...  60 us
    reduce_scatter x1, waiting for transfers between devices, body(): lax.psum_scatter(grad_qkv.astype(jnp.bfloat16), 'fsdp', scatter_dimension...  50.4 us
    all_gather x1, waiting for transfers between devices, body(): lax.all_gather(key_rows, 'ctx', axis=0, tiled=True)  46.1 us
    unnamed x132, local copies, waits for them, and re-layouts  42.1 us
    dynamic_slice x32, local copies, waits for them, and re-layouts, over_blocks(): lax.scan(scan_body, status, (jnp.arange(block_total, dtype=jnp.int32), st...  41.7 us
    psum x1, waiting for transfers between devices, body(): lax.psum(sum_qkv.astype(jnp.bfloat16), 'ctx').astype(jnp.float32)  40.5 us
  transfers between devices with their start and end apart: 12, of which 10 were waited for; matrix products, arithmetic and copies ran while one was open for 19% of the time, Pallas kernels for 0%

commit v1 on v0

--- a/solution.py
+++ b/solution.py
@@ -1,6 +1,10 @@
+import functools
+
 import jax
 import jax.numpy as jnp
 from jax import lax
+from jax.experimental import pallas as pl
+from jax.experimental.pallas import tpu as pltpu
 from jax.sharding import PartitionSpec as P
 
 HEADS = 12
@@ -96,7 +100,7 @@
     return (probabilities.astype(jnp.bfloat16), grad_scores)
 
 
-def body(
+def general_body(
     tokens,
     cotangent,
     w_qkv,
@@ -417,6 +421,568 @@
     )
 
 
+FP32 = jnp.float32
+BF16 = jnp.bfloat16
+FLOOR = -1e30
+NEVER = 1 << 30
+
+
+def dot_nt(left_side, right_side):
+    return lax.dot_general(
+        left_side, right_side, (((1,), (1,)), ((), ())), preferred_element_type=FP32
+    )
+
+
+def dot_nn(left_side, right_side):
+    return lax.dot_general(
+        left_side, right_side, (((1,), (0,)), ((), ())), preferred_element_type=FP32
+    )
+
+
+def spread(column_tile, width):
+    return jnp.concatenate([column_tile] * (width // column_tile.shape[1]), axis=1)
+
+
+def masked_scores(scores, key_ids, first_row, last_row):
+    permitted = key_ids >= first_row
+    if last_row is not None:
+        permitted = permitted & (key_ids <= last_row)
+    return jnp.where(permitted, scores, -jnp.inf)
+
+
+def attend_kernel(
+    parity, q_ref, k_ref, vt_ref, key_ref, low_ref, high_ref, far_ref, o_ref, ot_ref, lse_ref, acc_ref
+):
+    blocks, rows, width = q_ref.shape
+    heads = width // 64
+
+    def query_block(index, unused):
+        queries = [q_ref[index, :, 64 * h : 64 * h + 64] for h in range(heads)]
+        acc_ref[...] = jnp.zeros_like(acc_ref)
+
+        def key_step(key_block, carry, first_row, last_row):
+            ids = spread(key_ref[key_block], rows)
+            result = []
+            for h in range(heads):
+                span = slice(64 * h, 64 * h + 64)
+                top, total = carry[h]
+                scores = dot_nt(k_ref[key_block, :, span], queries[h])
+                scores = masked_scores(scores, ids, first_row, last_row)
+                new_top = jnp.maximum(top, jnp.max(scores, axis=0, keepdims=True))
+                fade = jnp.exp(top - new_top)
+                weights = jnp.exp(scores - new_top)
+                total = total * fade + jnp.sum(weights, axis=0, keepdims=True)
+                acc_ref[span, :] = acc_ref[span, :] * fade + dot_nn(
+                    vt_ref[key_block, span, :], weights.astype(BF16)
+                )
+                result.append((new_top, total))
+            return tuple(result)
+
+        start = tuple(
+            (jnp.full((1, rows), FLOOR, FP32), jnp.zeros((1, rows), FP32)) for h in range(heads)
+        )
+        own = 2 * index + parity[0]
+        far_row = far_ref[index]
+        carry = lax.fori_loop(
+            0, own, lambda j, c: key_step(j, c, far_row, None), start
+        )
+        carry = key_step(own, carry, low_ref[index], high_ref[index])
+        for h in range(heads):
+            span = slice(64 * h, 64 * h + 64)
+            top, total = carry[h]
+            attended = acc_ref[span, :] / total
+            ot_ref[index, span, :] = attended
+            o_ref[index, :, span] = attended.T.astype(BF16)
+            lse_ref[index, h : h + 1, :] = top + jnp.log(total)
+        return unused
+
+    lax.fori_loop(0, blocks, query_block, 0)
+
+
+def attend_back_kernel(
+    parity,
+    q_ref,
+    k_ref,
+    kt_ref,
+    v_ref,
+    da_ref,
+    key_ref,
+    low_ref,
+    high_ref,
+    far_ref,
+    ot_ref,
+    lse_ref,
+    dq_ref,
+    keep_ref,
+    send_ref,
+    acc_ref,
+    dk_ref,
+    dv_ref,
+):
+    blocks, rows, width = q_ref.shape
+    heads = width // 64
+    dk_ref[...] = jnp.zeros_like(dk_ref)
+    dv_ref[...] = jnp.zeros_like(dv_ref)
+
+    def query_block(index, unused):
+        queries = [q_ref[index, :, 64 * h : 64 * h + 64] for h in range(heads)]
+        grads = [da_ref[index, :, 64 * h : 64 * h + 64] for h in range(heads)]
+        deltas = [
+            jnp.sum(
+                grads[h].astype(FP32).T * ot_ref[index, 64 * h : 64 * h + 64, :],
+                axis=0,
+                keepdims=True,
+            )
+            for h in range(heads)
+        ]
+        logs = [lse_ref[index, h : h + 1, :] for h in range(heads)]
+        acc_ref[...] = jnp.zeros_like(acc_ref)
+
+        def key_step(key_block, first_row, last_row):
+            ids = spread(key_ref[key_block], rows)
+            for h in range(heads):
+                span = slice(64 * h, 64 * h + 64)
+                scores = dot_nt(k_ref[key_block, :, span], queries[h])
+                scores = masked_scores(scores, ids, first_row, last_row)
+                weights = jnp.exp(scores - logs[h])
+                slopes = dot_nt(v_ref[key_block, :, span], grads[h])
+                dscores = (weights * (slopes - deltas[h])).astype(BF16)
+                dv_ref[h, key_block] += dot_nn(weights.astype(BF16), grads[h])
+                dk_ref[h, key_block] += dot_nn(dscores, queries[h])
+                acc_ref[span, :] += dot_nn(kt_ref[key_block, span, :], dscores)
+
+        own = 2 * index + parity[0]
+        far_row = far_ref[index]
+
+        def far_step(key_block, state):
+            key_step(key_block, far_row, None)
+            return state
+
+        lax.fori_loop(0, own, far_step, 0)
+        key_step(own, low_ref[index], high_ref[index])
+        for h in range(heads):
+            span = slice(64 * h, 64 * h + 64)
+            dq_ref[index, :, span] = (acc_ref[span, :] * 0.125).T.astype(BF16)
+        return unused
+
+    lax.fori_loop(0, blocks, query_block, 0)
+
+    def write_block(index, unused):
+        mine = 2 * index + parity[0]
+        theirs = 2 * index + 1 - parity[0]
+        for h in range(heads):
+            left = slice(64 * h, 64 * h + 64)
+            right = slice(width + 64 * h, width + 64 * h + 64)
+            keep_ref[index, :, left] = dk_ref[h, mine]
+            keep_ref[index, :, right] = dv_ref[h, mine]
+            send_ref[index, :, left] = dk_ref[h, theirs].astype(BF16)
+            send_ref[index, :, right] = dv_ref[h, theirs].astype(BF16)
+        return unused
+
+    lax.fori_loop(0, blocks, write_block, 0)
+
+
+def kernel_call(kernel, outputs, scratch, operands, flops):
+    in_specs = [pl.BlockSpec(memory_space=pltpu.SMEM)] + [
+        pl.BlockSpec(memory_space=pltpu.VMEM) for unused in operands[1:]
+    ]
+    moved = sum(v.size * v.dtype.itemsize for v in list(operands) + list(outputs))
+    return pl.pallas_call(
+        kernel,
+        out_shape=outputs,
+        in_specs=in_specs,
+        out_specs=[pl.BlockSpec(memory_space=pltpu.VMEM) for unused in outputs],
+        scratch_shapes=scratch,
+        compiler_params=pltpu.CompilerParams(vmem_limit_bytes=56 * 1024 * 1024),
+        cost_estimate=pl.CostEstimate(flops=flops, bytes_accessed=moved, transcendentals=flops // 256),
+    )(*operands)
+
+
+def fast_body(
+    tokens,
+    cotangent,
+    w_qkv,
+    b_query,
+    b_value,
+    w_out,
+    b_out,
+    w_fc,
+    b_fc,
+    w_proj,
+    b_proj,
+    gain1,
+    shift1,
+    gain2,
+    shift2,
+    counts,
+    seq_lengths,
+):
+    rows, features = tokens.shape
+    ctx = lax.axis_size("ctx")
+    fsdp = lax.axis_size("fsdp")
+    chips = ctx // 2
+    group_heads = HEADS // chips
+    width = features // chips
+    shard = features // fsdp
+    hidden_width = w_fc.shape[1]
+    place = lax.axis_index("ctx")
+    chip = place // 2
+    core = place % 2
+    part = lax.axis_index("fsdp")
+    near = 1 + core
+    across = 2 - core
+
+    def exchange(value, partner):
+        pairs = [
+            (f * ctx + c, g * ctx + d)
+            for f in range(fsdp)
+            for c in range(ctx)
+            for g, d in [partner(f, c)]
+        ]
+        return jax.tree.map(lambda leaf: lax.ppermute(leaf, ("fsdp", "ctx"), pairs), value)
+
+    def to_near(value):
+        return exchange(value, lambda f, c: (f ^ (1 + c % 2), c))
+
+    def to_across(value):
+        return exchange(value, lambda f, c: (f ^ (2 - c % 2), c))
+
+    def to_part(value, step):
+        return exchange(value, lambda f, c: (f ^ step, c))
+
+    def to_core(value):
+        return exchange(value, lambda f, c: (f, c ^ 1))
+
+    def to_chip(value, step):
+        return exchange(value, lambda f, c: (f, c ^ (2 * step)))
+
+    def pick(array, index, axis=0):
+        return lax.dynamic_index_in_dim(array, index, axis, keepdims=False)
+
+    def place_all(shape, dtype, items):
+        buffer = jnp.zeros(shape, dtype)
+        for index, value in items:
+            full = value.reshape((1,) * (len(shape) - value.ndim) + value.shape)
+            starts = tuple(index) + (0,) * (len(shape) - len(index))
+            buffer = lax.dynamic_update_slice(buffer, full.astype(dtype), starts)
+        return buffer
+
+    def gather_weight(weight):
+        half = weight.shape[0] // 2
+        mine = lax.dynamic_slice_in_dim(weight, core * half, half, 0)
+        from_near = to_near(mine)
+        from_across = to_across(mine)
+        from_far = to_across(from_near)
+        other_near = to_core(from_across)
+        other_across = to_core(from_near)
+        other_far = to_core(from_far)
+        items = [
+            ((part ^ near, core), from_near),
+            ((part ^ across, core), from_across),
+            ((part ^ 3, core), from_far),
+            ((part ^ near, 1 - core), other_near),
+            ((part ^ across, 1 - core), other_across),
+            ((part ^ 3, 1 - core), other_far),
+            ((part, 0), weight.reshape(2, half, -1)),
+        ]
+        full = place_all((fsdp, 2, half, weight.shape[1]), weight.dtype, items)
+        return full.reshape(fsdp * weight.shape[0], weight.shape[1])
+
+    count_row = counts[0]
+    offsets = jnp.cumsum(count_row) - count_row
+    seq_ends = jnp.cumsum(seq_lengths[0])
+    within = jnp.arange(rows, dtype=jnp.int32)
+    slot = jnp.arange(ctx, dtype=jnp.int32)[:, None] * rows + within[None, :]
+    live = within[None, :] < count_row[:, None]
+    places = offsets[:, None] + within[None, :]
+    starts = jnp.max(
+        jnp.where(places[:, :, None] >= seq_ends[None, None, :], seq_ends[None, None, :], 0), axis=2
+    )
+    dead_id = -1 - slot
+    key_ids = jnp.where(live, places, dead_id)
+    lows = jnp.where(live, starts, dead_id)
+    highs = key_ids
+    fars = jnp.where(live, starts, NEVER)
+    key_tile = jnp.broadcast_to(key_ids[:, :, None], (ctx, rows, 128))
+
+    def own_parity(array):
+        return pick(array.reshape((chips, 2) + array.shape[1:]), core, 1)
+
+    low_rows = own_parity(lows)[:, None, :]
+    high_rows = own_parity(highs)[:, None, :]
+    far_rows = own_parity(fars)[:, None, :]
+    live_rows = (within < pick(count_row, place)).astype(FP32)[:, None]
+
+    smalls = jnp.concatenate(
+        [b_query, b_value, b_out, b_proj, gain1, shift1, gain2, shift2, b_fc]
+    ).reshape(-1, 128)
+    small_all = place_all(
+        (fsdp,) + smalls.shape,
+        BF16,
+        [((part,), smalls)] + [((part ^ s,), to_part(smalls, s)) for s in (1, 2, 3)],
+    )
+    small_all = small_all.reshape(fsdp, -1).astype(FP32)
+    vectors = [small_all[:, n * shard : (n + 1) * shard].reshape(-1) for n in range(8)]
+    bias_q, bias_v, bias_out, bias_proj, gain_one, shift_one, gain_two, shift_two = vectors
+    bias_fc = small_all[:, 8 * shard :].reshape(-1)
+
+    from_chips = [to_chip(tokens, s) for s in (1, 2, 3)]
+    beside = [to_core(tokens)] + [to_core(v) for v in from_chips]
+    tokens_all = place_all(
+        (chips, 2, rows, features),
+        BF16,
+        [((chip, core), tokens), ((chip, 1 - core), beside[0])]
+        + [((chip ^ s, core), from_chips[s - 1]) for s in (1, 2, 3)]
+        + [((chip ^ s, 1 - core), beside[s]) for s in (1, 2, 3)],
+    ).reshape(ctx, rows, features)
+
+    qkv_full = gather_weight(w_qkv)
+    out_full = gather_weight(w_out)
+    fc_full = gather_weight(w_fc)
+    proj_full = gather_weight(w_proj)
+    qkv_parts = jnp.transpose(
+        qkv_full.reshape(features, 3, chips, width), (2, 0, 1, 3)
+    ).reshape(chips, features, 3 * width)
+
+    wide_all = tokens_all.reshape(ctx * rows, features).astype(FP32)
+    normed_all = layer_norm(wide_all, gain_one, shift_one)[0].astype(BF16)
+    own_weight = pick(qkv_parts, chip)
+    own_bias_q = lax.dynamic_slice_in_dim(bias_q, chip * width, width, 0)
+    own_bias_v = lax.dynamic_slice_in_dim(bias_v, chip * width, width, 0)
+    weight_q, weight_k, weight_v = (own_weight[:, n * width : (n + 1) * width] for n in range(3))
+    normed_blocks = normed_all.reshape(ctx, rows, features)
+    normed_mine = own_parity(normed_blocks)
+    queries = dot_nn(normed_mine.reshape(chips * rows, features), weight_q) + own_bias_q
+    queries = (queries.astype(BF16) * jnp.asarray(0.125, BF16)).reshape(chips, rows, width)
+    keys = dot_nn(normed_all, weight_k).astype(BF16).reshape(ctx, rows, width)
+    values = (dot_nn(normed_all, weight_v) + own_bias_v).astype(BF16).reshape(ctx, rows, width)
+    keys_t = jnp.transpose(keys, (0, 2, 1))
+    values_t = jnp.transpose(values, (0, 2, 1))
+    parity = core.astype(jnp.int32).reshape(1)
+
+    pair_count = group_heads * rows * rows * (chips * (chips + 1))
+    attended_out, attended_t, logs = kernel_call(
+        attend_kernel,
+        [
+            jax.ShapeDtypeStruct((chips, rows, width), BF16),
+            jax.ShapeDtypeStruct((chips, width, rows), FP32),
+            jax.ShapeDtypeStruct((chips, 8, rows), FP32),
+        ],
+        [pltpu.VMEM((width, rows), FP32)],
+        (parity, queries, keys, values_t, key_tile, low_rows, high_rows, far_rows),
+        pair_count * 256,
+    )
+
+    def scatter_chips(blocks):
+        arrived = [(chip, pick(blocks, chip))]
+        for s in (1, 2, 3):
+            arrived.append((chip ^ s, to_chip(pick(blocks, chip ^ s), s)))
+        return arrived
+
+    attended_low = place_all(
+        (chips, rows, width), BF16, [((n,), v) for n, v in scatter_chips(attended_out)]
+    )
+    attended_low = jnp.transpose(attended_low, (1, 0, 2)).reshape(rows, features)
+
+    inputs = tokens.astype(FP32)
+    middle = inputs + dot_nn(attended_low, out_full) + bias_out
+    normed_two, unit_two, inverse_two = layer_norm(middle, gain_two, shift_two)
+    normed_two_low = normed_two.astype(BF16)
+    hidden = dot_nn(normed_two_low, fc_full) + bias_fc
+    activated = gelu_tanh(hidden).astype(BF16)
+    output_low = (middle + dot_nn(activated, proj_full) + bias_proj).astype(BF16)
+
+    grad_out = cotangent.astype(FP32) * live_rows
+    grad_out_low = grad_out.astype(BF16)
+    grad_act = times_transpose(grad_out_low, proj_full)
+    grad_hidden = jax.vjp(gelu_tanh, hidden)[1](grad_act)[0]
+    grad_hidden_low = grad_hidden.astype(BF16)
+    grad_normed_two = times_transpose(grad_hidden_low, fc_full)
+    grad_mid_norm, grad_gain_two, grad_shift_two = norm_back(
+        grad_normed_two, unit_two, inverse_two, gain_two
+    )
+    grad_middle = grad_out + grad_mid_norm
+    grad_middle_low = grad_middle.astype(BF16)
+    grad_attended = times_transpose(grad_middle_low, out_full).astype(BF16)
+    grad_heads = jnp.transpose(grad_attended.reshape(rows, chips, width), (1, 0, 2))
+    grad_blocks = place_all(
+        (chips, rows, width), BF16, [((n,), v) for n, v in scatter_chips(grad_heads)]
+    )
+
+    grad_query, grad_keep, grad_send = kernel_call(
+        attend_back_kernel,
+        [
+            jax.ShapeDtypeStruct((chips, rows, width), BF16),
+            jax.ShapeDtypeStruct((chips, rows, 2 * width), FP32),
+            jax.ShapeDtypeStruct((chips, rows, 2 * width), BF16),
+        ],
+        [
+            pltpu.VMEM((width, rows), FP32),
+            pltpu.VMEM((group_heads, ctx, rows, 64), FP32),
+            pltpu.VMEM((group_heads, ctx, rows, 64), FP32),
+        ],
+        (
+            parity,
+            queries,
+            keys,
+            keys_t,
+            values,
+            grad_blocks,
+            key_tile,
+            low_rows,
+            high_rows,
+            far_rows,
+            attended_t,
+            logs,
+        ),
+        pair_count * 640,
+    )
+    grad_kv = (grad_keep + to_core(grad_send).astype(FP32)).astype(BF16)
+    grad_packed = jnp.concatenate([grad_query, grad_kv], axis=2)
+
+    grad_normed_one = jnp.zeros((rows, features), FP32)
+    for source, piece in scatter_chips(grad_packed):
+        grad_normed_one = grad_normed_one + times_transpose(piece, pick(qkv_parts, source))
+    normed_one, unit_one, inverse_one = layer_norm(inputs, gain_one, shift_one)
+    grad_in_norm = norm_back(grad_normed_one, unit_one, inverse_one, gain_one)[0]
+    grad_tokens = grad_middle + grad_in_norm
+
+    def add_up(left_side, right_side):
+        return left_side.astype(FP32) + right_side.astype(FP32)
+
+    def scatter_parts(blocks):
+        theirs = to_near(pick(blocks, part ^ near).astype(BF16))
+        theirs_far = to_near(pick(blocks, part ^ 3).astype(BF16))
+        relay = add_up(pick(blocks, part ^ across), theirs_far).astype(BF16)
+        last = to_across(relay)
+        return pick(blocks, part).astype(FP32) + theirs.astype(FP32) + last.astype(FP32)
+
+    def sum_chips(block):
+        quarter = block.shape[0] // chips
+        quarters = block.astype(BF16).reshape((chips, quarter) + block.shape[1:])
+        total = pick(block.reshape((chips, quarter) + block.shape[1:]), chip).astype(FP32)
+        for s in (1, 2, 3):
+            total = total + to_chip(pick(quarters, chip ^ s), s).astype(FP32)
+        total = total.astype(BF16)
+        full = place_all(
+            quarters.shape,
+            BF16,
+            [((chip,), total)] + [((chip ^ s,), to_chip(total, s)) for s in (1, 2, 3)],
+        )
+        return full.reshape(block.shape)
+
+    other_grad_out = to_core(grad_out_low)
+    other_normed_two = to_core(normed_two_low)
+    other_attended = to_core(attended_low)
+    split_act = activated.reshape(rows, fsdp, 2, hidden_width // (2 * fsdp))
+    split_hidden = grad_hidden_low.reshape(rows, 2, hidden_width // 2)
+    split_middle = grad_middle_low.reshape(rows, 2, features // 2)
+    other_act = to_core(pick(split_act, 1 - core, 2).reshape(rows, -1))
+    other_hidden = to_core(pick(split_hidden, 1 - core, 1))
+    other_middle = to_core(pick(split_middle, 1 - core, 1))
+
+    def both(mine, other, mine_grad, other_grad):
+        return contract_rows(mine, mine_grad) + contract_rows(other, other_grad)
+
+    grad_proj = both(
+        pick(split_act, core, 2).reshape(rows, -1), other_act, grad_out_low, other_grad_out
+    ).reshape(fsdp, -1, features)
+    grad_fc = both(
+        normed_two_low, other_normed_two, pick(split_hidden, core, 1), other_hidden
+    ).reshape(fsdp, shard, -1)
+    grad_out_proj = both(
+        attended_low, other_attended, pick(split_middle, core, 1), other_middle
+    ).reshape(fsdp, shard, -1)
+    sums = [
+        jnp.sum(grad_middle_low.astype(FP32), axis=0),
+        jnp.sum(grad_out, axis=0),
+        grad_gain_two,
+        grad_shift_two,
+        jnp.sum(grad_hidden_low.astype(FP32), axis=0),
+    ]
+    sum_rows = jnp.concatenate([v.reshape(fsdp, -1) for v in sums], axis=1)
+    sum_rows = sum_rows.reshape(fsdp, -1, features // 2)
+    pad_rows = shard // 3 - sum_rows.shape[1]
+    grad_out_proj = jnp.concatenate(
+        [grad_out_proj, jnp.pad(sum_rows, ((0, 0), (0, pad_rows), (0, 0)))], axis=1
+    )
+    proj_half = sum_chips(scatter_parts(grad_proj))
+    fc_half = sum_chips(scatter_parts(grad_fc))
+    out_half = sum_chips(scatter_parts(grad_out_proj))
+    proj_other, fc_other, out_other = to_core(proj_half), to_core(fc_half), to_core(out_half)
+
+    def by_core(mine, other, axis):
+        first = jnp.where(core == 0, mine, other)
+        second = jnp.where(core == 0, other, mine)
+        return jnp.concatenate([first, second], axis=axis).astype(FP32)
+
+    d_proj = by_core(proj_half, proj_other, 0)
+    d_fc = by_core(fc_half, fc_other, 1)
+    d_out = by_core(out_half[:shard], out_other[:shard], 1)
+    small_sums = add_up(out_half[shard:], out_other[shard:]).reshape(-1)
+    d_bias_out, d_bias_proj, d_gain_two, d_shift_two = (
+        small_sums[n * shard : (n + 1) * shard] for n in range(4)
+    )
+    d_bias_fc = small_sums[4 * shard : 4 * shard + hidden_width // fsdp]
+
+    grad_qkv = contract_rows(
+        normed_mine.reshape(chips * rows, features), grad_packed.reshape(chips * rows, -1)
+    )
+    column_sums = jnp.sum(grad_packed.astype(FP32), axis=(0, 1))
+    own_wide = own_weight.astype(FP32)
+    grad_shift_one = jnp.sum(own_wide * column_sums[None, :], axis=1)
+    grad_gain_one = (jnp.sum(own_wide * grad_qkv, axis=1) - shift_one * grad_shift_one) / gain_one
+    half = shard // 2
+    split_qkv = grad_qkv.reshape(fsdp, 2, half, -1)
+    other_qkv = to_core(pick(split_qkv, 1 - core, 1).astype(BF16))
+    qkv_blocks = add_up(pick(split_qkv, core, 1), other_qkv)
+    norm_rows = jnp.concatenate(
+        [
+            grad_gain_one.reshape(fsdp, shard),
+            grad_shift_one.reshape(fsdp, shard),
+            jnp.zeros((fsdp, 3 * width - 2 * shard), FP32),
+        ],
+        axis=1,
+    )
+    extra = jnp.stack([jnp.broadcast_to(column_sums, (fsdp, 3 * width)), norm_rows], axis=1)
+    qkv_blocks = jnp.concatenate([qkv_blocks, jnp.pad(extra, ((0, 0), (0, 14), (0, 0)))], axis=1)
+    qkv_half = scatter_parts(qkv_blocks).astype(BF16)
+    qkv_pieces = [((chip, core), qkv_half)]
+    qkv_pieces += [((chip ^ s, core), to_chip(qkv_half, s)) for s in (1, 2, 3)]
+    qkv_pieces += [((index[0], 1 - core), to_core(v)) for index, v in qkv_pieces]
+    qkv_total = place_all((chips, 2) + qkv_half.shape, BF16, qkv_pieces)
+    d_qkv = jnp.transpose(
+        qkv_total[:, :, :half].reshape(chips, 2, half, 3, width), (1, 2, 3, 0, 4)
+    )
+    d_qkv = d_qkv.reshape(shard, 3 * features).astype(FP32)
+    extra_total = jnp.sum(qkv_total[:, :, half : half + 2].astype(FP32), axis=1)
+    bias_total = extra_total[:, 0].reshape(chips, 3, width)
+    bias_total = jnp.transpose(bias_total, (1, 0, 2)).reshape(3, features)
+    d_bias_q = lax.dynamic_slice_in_dim(bias_total[0], part * shard, shard, 0)
+    d_bias_v = lax.dynamic_slice_in_dim(bias_total[2], part * shard, shard, 0)
+    norm_total = jnp.sum(extra_total[:, 1], axis=0)
+    d_gain_one = norm_total[:shard]
+    d_shift_one = norm_total[shard : 2 * shard]
+
+    return (
+        output_low,
+        grad_tokens,
+        d_qkv,
+        d_bias_q,
+        d_bias_v,
+        d_out,
+        d_bias_out,
+        d_fc,
+        d_bias_fc,
+        d_proj,
+        d_bias_proj,
+        d_gain_one,
+        d_shift_one,
+        d_gain_two,
+        d_shift_two,
+    )
+
+
 def solution(mesh):
     in_specs = (
         P(("fsdp", "ctx"), None),
@@ -454,4 +1020,7 @@
         P("fsdp"),
         P("fsdp"),
     )
+    ctx = mesh.shape["ctx"]
+    four_by_four = mesh.shape["fsdp"] == 4 and ctx == 8 and HEADS % (ctx // 2) == 0
+    body = fast_body if four_by_four else general_body
     return jax.shard_map(body, mesh=mesh, in_specs=in_specs, out_specs=out_specs, check_vma=False)

time: 907 us -> 619 us (0.68)
  waiting for transfers between devices: 454 us -> 141 us
  starting transfers between devices: 0.48 us -> 113 us
  matrix products: 145 us -> 66.6 us
  local copies, waits for them, and re-layouts: 104 us -> 178 us
  other arithmetic: 112 us -> 53.3 us
  blocking collectives: 57 us -> 0 us
  Pallas kernels: 0 us -> 55.5 us
  between operations: 17 us -> 2.53 us
  loops' own time: 12.2 us -> 0 us
    reduce_scatter x4 -> x0, waiting for transfers between devices: 183 us -> none  [the longest x1 60.1 us: body(): lax.psum_scatter(grad_fc.astype(jnp.bfloat16), 'fsdp', scatter_dimension=...]
    all_gather x6 -> x0, waiting for transfers between devices: 146 us -> none  [the longest x1 46.1 us: body(): lax.all_gather(key_rows, 'ctx', axis=0, tiled=True)]
    ppermute x0 -> x91, waiting for transfers between devices: none -> 141 us  [exchange(): lax.ppermute(leaf, ('fsdp', 'ctx'), pairs)]
    ppermute x0 -> x91, starting transfers between devices: none -> 113 us  [exchange(): lax.ppermute(leaf, ('fsdp', 'ctx'), pairs)]
    unnamed x13 -> x0, waiting for transfers between devices: 84 us -> none
    dot_general x60 -> x6, matrix products: 107 us -> 25.6 us  [dot_nn(): lax.dot_general(left_side, right_side, (((1,), (0,)), ((), ())), preferre...]
    pallas_call x0 -> x2, Pallas kernels: none -> 55.5 us  [kernel_call(): pl.pallas_call(kernel, out_shape=outputs, in_specs=in_specs, out_specs=[p...]
    dynamic_update_slice x0 -> x63, local copies, waits for them, and re-layouts: none -> 42.1 us  [place_all(): buffer = lax.dynamic_update_slice(buffer, full.astype(dtype), starts)]
  transfers between devices with their start and end apart: 12 -> 91, of which waited for: 10 -> 29; matrix products, arithmetic and copies ran while one was open for 19% -> 47% of each run, Pallas kernels for 0% -> 9%
where the time goes in v1:
time: 619 us; the launch traced here: 610 us
  local copies, waits for them, and re-layouts  178 us (29%)
  waiting for transfers between devices  141 us (23%)
  starting transfers between devices  113 us (18%)
  matrix products  66.6 us (11%)
  Pallas kernels  55.5 us (9%)
  other arithmetic  53.3 us (9%)
    ppermute x91, waiting for transfers between devices, exchange(): lax.ppermute(leaf, ('fsdp', 'ctx'), pairs)  141 us
    ppermute x91, starting transfers between devices, exchange(): lax.ppermute(leaf, ('fsdp', 'ctx'), pairs)  113 us
    pallas_call x2, Pallas kernels, kernel_call(): pl.pallas_call(kernel, out_shape=outputs, in_specs=in_specs, out_specs=[p...  55.5 us
    dynamic_update_slice x63, local copies, waits for them, and re-layouts, place_all(): buffer = lax.dynamic_update_slice(buffer, full.astype(dtype), starts)  42.1 us
    dot_general x6, matrix products, dot_nn(): lax.dot_general(left_side, right_side, (((1,), (0,)), ((), ())), preferre...  25.6 us
    dot_general x7, matrix products, times_transpose(): lax.dot_general(left_side, right_side, (((1,), (1,)), ((), ())), preferre...  20.6 us
    dot_general x7, matrix products, contract_rows(): lax.dot_general(left_side, right_side, (((0,), (0,)), ((), ())), preferre...  20.4 us
    unnamed x115, local copies, waits for them, and re-layouts  19 us
  transfers between devices with their start and end apart: 91, of which 29 were waited for; matrix products, arithmetic and copies ran while one was open for 47% of the time, Pallas kernels for 9%

profile of v1, /device:TPU:0, one launch (start us, length us, event | category | flops | bytes accessed | tf_op | source)
XLA Modules:
  0.0 610.1 jit_solution(13660275254088845819)
XLA Ops:
  0.7 6.8 %concatenate.27 = bf16[2304]{0:T(1024)(128)(2,1)} concatenate(bf16[192]{0:T(256)(128)(2,1)} %param.20, bf16[192]{0:T(256)(128)(2,1)} %param.21, bf16[192]{0:T(256)(128)(2,1)} %param.23, bf16[192]{0:T(256)(128)(2,1)} %param.27, bf16[192]{0:T(256)(128)(2,1)} %param.28, bf16[192]{0:T(256)(128)(2,1)} %param.29, bf16[192]{0:T(256)(128)(2,1)} %param.30, bf16[192]{0:T(256)(128)(2,1)} %param.31, ...), dimensions={0} | concatenate | bytes 9216 | tf_op jit(solution)/shard_map/concatenate | solution.py:716
  7.5 2.9 collective-permute-start.7
  31.8 2.4 broadcast.240.clone.1
  51.1 3.4 collective-permute-done.21
  66.2 4.1 collective-permute-done.11
  72.6 7.6 %collective-permute-done.25 = bf16[96,3072]{1,0:T(8,128)(2,1)S(1)} collective-permute-done((bf16[96,3072]{1,0:T(8,128)(2,1)S(1)}, bf16[96,3072]{1,0:T(8,128)(2,1)S(1)}, u32[]{:S(2)}, u32[]{:S(2)}) %collective-permute-start.25) | collective-permute-done | bytes 589856 | tf_op jit(solution)/shard_map/ppermute | solution.py:642
  81.6 2.7 broadcast_in_dim.40
  85.2 4.8 collective-permute-done.26
  90.0 2.6 collective-permute-start.2
  93.5 2.5 broadcast.240.clone
  103.3 25.3 %collective-permute-done.2 = bf16[384,768]{1,0:T(8,128)(2,1)S(1)} collective-permute-done((bf16[384,768]{1,0:T(8,128)(2,1)S(1)}, bf16[384,768]{1,0:T(8,128)(2,1)S(1)}, u32[]{:S(2)}, u32[]{:S(2)}) %collective-permute-start.2) | collective-permute-done | bytes 589856 | tf_op jit(solution)/shard_map/ppermute | solution.py:642
  136.2 9.6 %collective-permute-done.27 = bf16[96,3072]{1,0:T(8,128)(2,1)} collective-permute-done((bf16[96,3072]{1,0:T(8,128)(2,1)S(1)}, bf16[96,3072]{1,0:T(8,128)(2,1)}, u32[]{:S(2)}, u32[]{:S(2)}) %collective-permute-start.27) | collective-permute-done | bytes 589856 | tf_op jit(solution)/shard_map/ppermute | solution.py:642
  158.4 10.1 %reshape_reshape.22 = bf16[768,3,4,192]{3,2,1,0:T(4,128)(2,1)} reshape(bf16[4,2,96,2304]{3,2,1,0:T(8,128)(2,1)} %constant_dynamic-update-slice_fusion.11) | data formatting | bytes 7077888 | tf_op jit(solution)/shard_map/reshape;reshape | solution.py:744
  168.5 8.1 %copy.132 = bf16[4,768,3,192]{1,3,2,0:T(8,128)(2,1)} copy(bf16[4,768,3,192]{3,0,2,1:T(4,128)(2,1)} %bitcast.394) | data formatting | bytes 7077888 | tf_op jit(solution)/shard_map/transpose | solution.py:743
  177.8 2.5 bitcast_dynamic-update-slice_fusion
  180.3 3.0 convert_reduce_fusion.1
  183.4 6.1 multiply_reduce_fusion
  189.6 3.0 fusion.13
  196.0 3.6 fusion.3
  203.9 5.1 fusion.14
  213.7 24.9 %shard_map.280 = (bf16[4,384,192]{2,1,0:T(8,128)(2,1)}, f32[4,192,384]{2,1,0:T(8,128)}, f32[4,8,384]{2,1,0:T(8,128)}) custom-call(s32[1]{0:T(128)} %bitcast.parity, bf16[4,384,192]{2,1,0:T(8,128)(2,1)} %bitcast.433, bf16[8,384,192]{2,1,0:T(8,128)(2,1)} %copy.135.k_ref, bf16[8,192,384]{2,1,0:T(8,128)(2,1)} %copy.136.vt_ref, ...), custom_call_target="tpu_custom_call" | custom-call | flops 2264924160 | bytes 6359044 | tf_op jit(solution)/shard_map/pallas_call | solution.py:590
  240.0 12.3 %collective-permute-start.16 = (bf16[384,192]{1,0:T(8,128)(2,1)S(1)}, bf16[384,192]{1,0:T(8,128)(2,1)S(1)}, u32[]{:S(2)}, u32[]{:S(2)}) collective-permute-start(bf16[384,192]{1,0:T(8,128)(2,1)S(1)} %get-tuple-element.80), channel_id=1, source_target_pairs={{0,2},{1,3},{2,0},{3,1},{4,6},{5,7},{6,4},{7,5},{8,10},{9,11},{10,... | collective-permute-start | bytes 442376 | tf_op jit(solution)/shard_map/ppermute | solution.py:642
  256.1 6.7 %fusion.118 = f32[384,3072]{1,0:T(8,128)} fusion(bf16[384,768]{1,0:T(8,128)(2,1)} %fusion.39, bf16[3072,768]{1,0:T(8,128)(2,1)} %bitcast.65), kind=kOutput, calls=%fused_computation.332 | convolution fusion | flops 1811939328 | bytes 10027008 | tf_op jit(solution)/shard_map/dot_general | solution.py:40
  268.3 2.4 fusion.117
  271.5 9.4 %convert_reduce_fusion = (f32[3072]{0:T(1024)}, bf16[384,3072]{1,0:T(8,128)(2,1)S(1)}, bf16[384,3072]{1,0:T(8,128)(2,1)}) fusion(f32[384,3072]{1,0:T(8,128)S(1)} %copy-done.49, f32[3072]{0:T(1024)S(1)} %copy-done.43, bf16[384,768]{1,0:T(8,128)(2,1)S(1)} %add_convert_fusion.1, bf16[768,3072]{1,0:T(8,128)(2,1)} %bitcast.57), kind=kOutput, calls=%fused_computation.19 | convolution fusion | flops 1841427456 | bytes 14770176 | tf_op jit(solution)/shard_map/dot_general | solution.py:437
  281.0 6.1 %multiply_reduce_fusion.1 = (f32[768]{0:T(1024)}, f32[384]{0:T(512)S(1)}, f32[384]{0:T(512)S(1)}, f32[768]{0:T(1024)S(1)}, f32[384,768]{1,0:T(8,128)S(1)}) fusion(f32[384,768]{1,0:T(8,128)S(1)} %get-tuple-element.121, f32[384]{0:T(512)S(1)} %add_rsqrt_fusion.2, f32[384]{0:T(512)S(1)} %broadcast_multiply_fusion.6, f32[768]{0:T(1024)S(1)} %copy-done.31, ...), kind=kOutput, calls=%fused_computation.100 | convolution fusion | flops 1814591232 | bytes 9452544 | tf_op jit(solution)/shard_map/dot_general | solution.py:40
  288.7 2.8 convolution_convert_fusion.1
  291.6 5.0 collective-permute-start.55
  296.7 6.0 reshape.763
  313.5 6.3 %constant_dynamic-slice_fusion.3 = (bf16[384,1,1536]{2,1,0:T(2,128)(2,1)}, bf16[384,1,1536]{2,1,0:T(2,128)(2,1)S(1)}) fusion(bf16[384,2,1536]{2,1,0:T(2,128)(2,1)S(1)} %reshape.763, s32[]{:T(128)S(6)} %select_n.303, s32[]{:T(128)S(6)} %select_n.302), kind=kLoop, calls=%fused_computation.258 | loop fusion | bytes 4718600 | tf_op jit(solution)/shard_map/jit(dynamic_index_in_dim)/dynamic_slice | solution.py:660
  319.8 3.6 fusion.33
  323.3 5.7 reshape.772
  329.1 7.1 %constant_dynamic-slice_fusion.1 = (bf16[384,4,1,384]{3,2,1,0:T(2,128)(2,1)}, bf16[384,4,1,384]{3,2,1,0:T(2,128)(2,1)}) fusion(bf16[384,4,2,384]{3,2,1,0:T(2,128)(2,1)S(1)} %reshape.772, s32[]{:T(128)S(6)} %select_n.303, s32[]{:T(128)S(6)} %select_n.302), kind=kLoop, calls=%fused_computation.256 | loop fusion | bytes 4718600 | tf_op jit(solution)/shard_map/jit(dynamic_index_in_dim)/dynamic_slice | solution.py:660
  336.2 5.6 copy.166
  341.8 4.7 fusion.119
  352.6 5.7 copy.167
  367.8 2.5 collective-permute-done.58
  371.9 4.8 collective-permute-done.38
  378.9 3.5 collective-permute-done.59
  384.6 2.3 collective-permute-start.60
  391.2 30.6 %shard_map.281 = (bf16[4,384,192]{2,1,0:T(8,128)(2,1)}, f32[4,384,384]{2,1,0:T(8,128)}, bf16[4,384,384]{2,1,0:T(8,128)(2,1)}) custom-call(s32[1]{0:T(128)} %bitcast.parity, bf16[4,384,192]{2,1,0:T(8,128)(2,1)} %bitcast.434, bf16[8,384,192]{2,1,0:T(8,128)(2,1)} %copy.135.k_ref, bf16[8,192,384]{2,1,0:T(8,128)(2,1)} %bitcast.431, ...), custom_call_target="tpu_custom_call" | custom-call | flops 5662310400 | bytes 11667460 | tf_op jit(solution)/shard_map/pallas_call | solution.py:590
  423.2 4.1 collective-permute-done.64
  429.3 3.8 collective-permute-done.65
  435.3 3.1 convolution_add_fusion.2
  441.8 2.9 convolution_add_fusion.1
  458.1 3.1 fusion.17
  462.3 6.2 %fusion.27 = bf16[384,768]{1,0:T(8,128)(2,1)} fusion(f32[384,768]{1,0:T(8,128)} %copy-done.5, bf16[384,3072]{1,0:T(8,128)(2,1)} %get-tuple-element.62, bf16[3072,768]{1,0:T(8,128)(2,1)} %bitcast.65, f32[768]{0:T(1024)S(1)} %add.551), kind=kOutput, calls=%fused_computation.69 | convolution fusion | flops 1812824064 | bytes 8850432 | tf_op jit(solution)/shard_map/dot_general | solution.py:437
  470.6 3.0 copy.145
  475.8 2.5 fusion.36
  478.3 2.4 collective-permute-start.41
  480.7 2.4 fusion.34
  487.0 15.2 %collective-permute-done.41 = bf16[384,576]{1,0:T(8,128)(2,1)S(1)} collective-permute-done((bf16[384,576]{1,0:T(8,128)(2,1)S(1)}, bf16[384,576]{1,0:T(8,128)(2,1)S(1)}, u32[]{:S(2)}, u32[]{:S(2)}) %collective-permute-start.41) | collective-permute-done | bytes 442400 | tf_op jit(solution)/shard_map/ppermute | solution.py:642
  502.9 9.9 %collective-permute-done.42 = bf16[384,576]{1,0:T(8,128)(2,1)} collective-permute-done((bf16[384,576]{1,0:T(8,128)(2,1)}, bf16[384,576]{1,0:T(8,128)(2,1)}, u32[]{:S(2)}, u32[]{:S(2)}) %collective-permute-start.42) | collective-permute-done | bytes 442400 | tf_op jit(solution)/shard_map/ppermute | solution.py:642
  515.4 4.6 collective-permute-done.47
  521.6 2.6 collective-permute-start.49
  526.9 7.5 %collective-permute-done.49 = bf16[112,576]{1,0:T(8,128)(2,1)S(1)} collective-permute-done((bf16[112,576]{1,0:T(8,128)(2,1)S(1)}, bf16[112,576]{1,0:T(8,128)(2,1)S(1)}, u32[]{:S(2)}, u32[]{:S(2)}) %collective-permute-start.49) | collective-permute-done | bytes 129056 | tf_op jit(solution)/shard_map/ppermute | solution.py:642
  542.1 4.4 copy.155
  546.5 3.7 reshape.785
  564.0 9.0 %collective-permute-start.84 = (bf16[96,768]{1,0:T(8,128)(2,1)S(1)}, bf16[96,768]{1,0:T(8,128)(2,1)S(1)}, u32[]{:S(2)}, u32[]{:S(2)}) collective-permute-start(bf16[96,768]{1,0:T(8,128)(2,1)S(1)} %get-tuple-element.83), channel_id=1, source_target_pairs={{0,2},{1,3},{2,0},{3,1},{4,6},{5,7},{6,4},{7,5},{8,10},{9,11},{10,... | collective-permute-start | bytes 442376 | tf_op jit(solution)/shard_map/ppermute | solution.py:642
  573.0 4.3 collective-permute-done.73
  577.5 2.5 collective-permute-start.76
  581.9 8.1 %collective-permute-done.85 = bf16[96,768]{1,0:T(8,128)(2,1)S(1)} collective-permute-done((bf16[96,768]{1,0:T(8,128)(2,1)S(1)}, bf16[96,768]{1,0:T(8,128)(2,1)S(1)}, u32[]{:S(2)}, u32[]{:S(2)}) %collective-permute-start.85) | collective-permute-done | bytes 147488 | tf_op jit(solution)/shard_map/ppermute | solution.py:642
  590.3 2.5 collective-permute-start.88
  595.8 10.0 %collective-permute-done.88 = bf16[96,768]{1,0:T(8,128)(2,1)S(1)} collective-permute-done((bf16[96,768]{1,0:T(8,128)(2,1)S(1)}, bf16[96,768]{1,0:T(8,128)(2,1)S(1)}, u32[]{:S(2)}, u32[]{:S(2)}) %collective-permute-start.88) | collective-permute-done | bytes 147488 | tf_op jit(solution)/shard_map/ppermute | solution.py:642
  (491 shorter events, 215.9 us)
Async XLA Ops:
  7.5 30.1 %collective-permute-start.7 = (bf16[18,128]{1,0:T(8,128)(2,1)}, bf16[18,128]{1,0:T(8,128)(2,1)}, u32[]{:S(2)}, u32[]{:S(2)}) collective-permute-start(bf16[18,128]{1,0:T(8,128)(2,1)} %bitcast.10), channel_id=1, source_target_pairs={{0,8},{1,9},{2,10},{3,11},{4,12},{5,13},{6,14},{7,15},{8,0},{9,1},... | collective-permute-start | bytes 13832 | tf_op jit(solution)/shard_map/ppermute | solution.py:642
  10.4 27.8 %collective-permute-start.8 = (bf16[18,128]{1,0:T(8,128)(2,1)}, bf16[18,128]{1,0:T(8,128)(2,1)}, u32[]{:S(2)}, u32[]{:S(2)}) collective-permute-start(bf16[18,128]{1,0:T(8,128)(2,1)} %bitcast.10), channel_id=1, source_target_pairs={{0,16},{1,17},{2,18},{3,19},{4,20},{5,21},{6,22},{7,23},{8,24},{9,... | collective-permute-start | bytes 13832 | tf_op jit(solution)/shard_map/ppermute | solution.py:642
  12.0 27.5 %collective-permute-start.9 = (bf16[18,128]{1,0:T(8,128)(2,1)}, bf16[18,128]{1,0:T(8,128)(2,1)}, u32[]{:S(2)}, u32[]{:S(2)}) collective-permute-start(bf16[18,128]{1,0:T(8,128)(2,1)} %bitcast.10), channel_id=1, source_target_pairs={{0,24},{1,25},{2,26},{3,27},{4,28},{5,29},{6,30},{7,31},{8,16},{9,... | collective-permute-start | bytes 13832 | tf_op jit(solution)/shard_map/ppermute | solution.py:642
  13.1 80.4 %collective-permute-start.31 = (bf16[384,768]{1,0:T(8,128)(2,1)S(1)}, bf16[384,768]{1,0:T(8,128)(2,1)S(1)}, u32[]{:S(2)}, u32[]{:S(2)}) collective-permute-start(bf16[384,768]{1,0:T(8,128)(2,1)S(1)} %constant_dynamic-slice_fusion.13), channel_id=1, source_target_pairs={{0,8},{1,17},{2,10},{3,19},{4,12},{5,21},{6,14},{7,23},{8,0},{9,25... | collective-permute-start | bytes 1769480 | tf_op jit(solution)/shard_map/ppermute | solution.py:642
  15.1 81.8 %collective-permute-start.32 = (bf16[384,768]{1,0:T(8,128)(2,1)S(1)}, bf16[384,768]{1,0:T(8,128)(2,1)}, u32[]{:S(2)}, u32[]{:S(2)}) collective-permute-start(bf16[384,768]{1,0:T(8,128)(2,1)S(1)} %constant_dynamic-slice_fusion.13), channel_id=1, source_target_pairs={{0,16},{1,9},{2,18},{3,11},{4,20},{5,13},{6,22},{7,15},{8,24},{9,1... | collective-permute-start | bytes 1769480 | tf_op jit(solution)/shard_map/ppermute | solution.py:642
  37.5 61.3 %collective-permute-start = (bf16[384,768]{1,0:T(8,128)(2,1)S(1)}, bf16[384,768]{1,0:T(8,128)(2,1)}, u32[]{:S(2)}, u32[]{:S(2)}) collective-permute-start(bf16[384,768]{1,0:T(8,128)(2,1)S(1)} %copy-done), channel_id=1, source_target_pairs={{0,1},{1,0},{2,3},{3,2},{4,5},{5,4},{6,7},{7,6},{8,9},{9,8},{10,11... | collective-permute-start | bytes 1769480 | tf_op jit(solution)/shard_map/ppermute | solution.py:642
  39.5 9.4 %collective-permute-start.20 = (bf16[96,768]{1,0:T(8,128)(2,1)S(1)}, bf16[96,768]{1,0:T(8,128)(2,1)S(1)}, u32[]{:S(2)}, u32[]{:S(2)}) collective-permute-start(bf16[96,768]{1,0:T(8,128)(2,1)S(1)} %constant_dynamic-slice_fusion.15), channel_id=1, source_target_pairs={{0,16},{1,9},{2,18},{3,11},{4,20},{5,13},{6,22},{7,15},{8,24},{9,1... | collective-permute-start | bytes 442376 | tf_op jit(solution)/shard_map/ppermute | solution.py:642
  45.1 16.6 %collective-permute-start.10 = (bf16[96,2304]{1,0:T(8,128)(2,1)}, bf16[96,2304]{1,0:T(8,128)(2,1)S(1)}, u32[]{:S(2)}, u32[]{:S(2)}) collective-permute-start(bf16[96,2304]{1,0:T(8,128)(2,1)} %constant_dynamic-slice_fusion.18), channel_id=1, source_target_pairs={{0,8},{1,17},{2,10},{3,19},{4,12},{5,21},{6,14},{7,23},{8,0},{9,25... | collective-permute-start | bytes 1327112 | tf_op jit(solution)/shard_map/ppermute | solution.py:642
  58.6 43.9 %collective-permute-start.1 = (bf16[384,768]{1,0:T(8,128)(2,1)S(1)}, bf16[384,768]{1,0:T(8,128)(2,1)S(1)}, u32[]{:S(2)}, u32[]{:S(2)}) collective-permute-start(bf16[384,768]{1,0:T(8,128)(2,1)S(1)} %copy-done), channel_id=1, source_target_pairs={{0,2},{1,3},{2,0},{3,1},{4,6},{5,7},{6,4},{7,5},{8,10},{9,11},{10,... | collective-permute-start | bytes 1769480 | tf_op jit(solution)/shard_map/ppermute | solution.py:642
  70.2 9.9 %collective-permute-start.25 = (bf16[96,3072]{1,0:T(8,128)(2,1)S(1)}, bf16[96,3072]{1,0:T(8,128)(2,1)S(1)}, u32[]{:S(2)}, u32[]{:S(2)}) collective-permute-start(bf16[96,3072]{1,0:T(8,128)(2,1)S(1)} %constant_dynamic-slice_fusion.14), channel_id=1, source_target_pairs={{0,8},{1,17},{2,10},{3,19},{4,12},{5,21},{6,14},{7,23},{8,0},{9,25... | collective-permute-start | bytes 1769480 | tf_op jit(solution)/shard_map/ppermute | solution.py:642
  80.1 9.9 %collective-permute-start.26 = (bf16[96,3072]{1,0:T(8,128)(2,1)S(1)}, bf16[96,3072]{1,0:T(8,128)(2,1)S(1)}, u32[]{:S(2)}, u32[]{:S(2)}) collective-permute-start(bf16[96,3072]{1,0:T(8,128)(2,1)S(1)} %constant_dynamic-slice_fusion.14), channel_id=1, source_target_pairs={{0,16},{1,9},{2,18},{3,11},{4,20},{5,13},{6,22},{7,15},{8,24},{9,1... | collective-permute-start | bytes 1769480 | tf_op jit(solution)/shard_map/ppermute | solution.py:642
  90.0 38.6 %collective-permute-start.2 = (bf16[384,768]{1,0:T(8,128)(2,1)S(1)}, bf16[384,768]{1,0:T(8,128)(2,1)S(1)}, u32[]{:S(2)}, u32[]{:S(2)}) collective-permute-start(bf16[384,768]{1,0:T(8,128)(2,1)S(1)} %copy-done), channel_id=1, source_target_pairs={{0,4},{1,5},{2,6},{3,7},{4,0},{5,1},{6,2},{7,3},{8,12},{9,13},{10,... | collective-permute-start | bytes 1769480 | tf_op jit(solution)/shard_map/ppermute | solution.py:642
  93.5 36.0 %collective-permute-start.3 = (bf16[384,768]{1,0:T(8,128)(2,1)S(1)}, bf16[384,768]{1,0:T(8,128)(2,1)S(1)}, u32[]{:S(2)}, u32[]{:S(2)}) collective-permute-start(bf16[384,768]{1,0:T(8,128)(2,1)S(1)} %copy-done), channel_id=1, source_target_pairs={{0,6},{1,7},{2,4},{3,5},{4,2},{5,3},{6,0},{7,1},{8,14},{9,15},{10,... | collective-permute-start | bytes 1769480 | tf_op jit(solution)/shard_map/ppermute | solution.py:642
  96.9 344.4 %collective-permute-start.80 = (bf16[384,768]{1,0:T(8,128)(2,1)}, bf16[384,768]{1,0:T(8,128)(2,1)}, u32[]{:S(2)}, u32[]{:S(2)}) collective-permute-start(bf16[384,768]{1,0:T(8,128)(2,1)} %fusion.39), channel_id=1, source_target_pairs={{0,1},{1,0},{2,3},{3,2},{4,5},{5,4},{6,7},{7,6},{8,9},{9,8},{10,11... | collective-permute-start | bytes 1769480 | tf_op jit(solution)/shard_map/ppermute | solution.py:642
  98.8 33.1 %collective-permute-start.12 = (bf16[96,2304]{1,0:T(8,128)(2,1)S(1)}, bf16[96,2304]{1,0:T(8,128)(2,1)S(1)}, u32[]{:S(2)}, u32[]{:S(2)}) collective-permute-start(bf16[96,2304]{1,0:T(8,128)(2,1)S(1)} %collective-permute-done.10), channel_id=1, source_target_pairs={{0,16},{1,9},{2,18},{3,11},{4,20},{5,13},{6,22},{7,15},{8,24},{9,1... | collective-permute-start | bytes 1327112 | tf_op jit(solution)/shard_map/ppermute | solution.py:642
  102.5 30.5 %collective-permute-start.13 = (bf16[96,2304]{1,0:T(8,128)(2,1)S(1)}, bf16[96,2304]{1,0:T(8,128)(2,1)S(1)}, u32[]{:S(2)}, u32[]{:S(2)}) collective-permute-start(bf16[96,2304]{1,0:T(8,128)(2,1)S(1)} %collective-permute-done.11), channel_id=1, source_target_pairs={{0,1},{1,0},{2,3},{3,2},{4,5},{5,4},{6,7},{7,6},{8,9},{9,8},{10,11... | collective-permute-start | bytes 1327112 | tf_op jit(solution)/shard_map/ppermute | solution.py:642
  129.5 21.6 %collective-permute-start.33 = (bf16[384,768]{1,0:T(8,128)(2,1)S(1)}, bf16[384,768]{1,0:T(8,128)(2,1)S(1)}, u32[]{:S(2)}, u32[]{:S(2)}) collective-permute-start(bf16[384,768]{1,0:T(8,128)(2,1)S(1)} %collective-permute-done.31), channel_id=1, source_target_pairs={{0,16},{1,9},{2,18},{3,11},{4,20},{5,13},{6,22},{7,15},{8,24},{9,1... | collective-permute-start | bytes 1769480 | tf_op jit(solution)/shard_map/ppermute | solution.py:642
  132.0 20.2 %collective-permute-start.34 = (bf16[384,768]{1,0:T(8,128)(2,1)}, bf16[384,768]{1,0:T(8,128)(2,1)S(1)}, u32[]{:S(2)}, u32[]{:S(2)}) collective-permute-start(bf16[384,768]{1,0:T(8,128)(2,1)} %collective-permute-done.32), channel_id=1, source_target_pairs={{0,1},{1,0},{2,3},{3,2},{4,5},{5,4},{6,7},{7,6},{8,9},{9,8},{10,11... | collective-permute-start | bytes 1769480 | tf_op jit(solution)/shard_map/ppermute | solution.py:642
  132.9 20.5 %collective-permute-start.35 = (bf16[384,768]{1,0:T(8,128)(2,1)S(1)}, bf16[384,768]{1,0:T(8,128)(2,1)S(1)}, u32[]{:S(2)}, u32[]{:S(2)}) collective-permute-start(bf16[384,768]{1,0:T(8,128)(2,1)S(1)} %collective-permute-done.31), channel_id=1, source_target_pairs={{0,1},{1,0},{2,3},{3,2},{4,5},{5,4},{6,7},{7,6},{8,9},{9,8},{10,11... | collective-permute-start | bytes 1769480 | tf_op jit(solution)/shard_map/ppermute | solution.py:642
  134.1 11.7 %collective-permute-start.27 = (bf16[96,3072]{1,0:T(8,128)(2,1)S(1)}, bf16[96,3072]{1,0:T(8,128)(2,1)}, u32[]{:S(2)}, u32[]{:S(2)}) collective-permute-start(bf16[96,3072]{1,0:T(8,128)(2,1)S(1)} %collective-permute-done.25), channel_id=1, source_target_pairs={{0,16},{1,9},{2,18},{3,11},{4,20},{5,13},{6,22},{7,15},{8,24},{9,1... | collective-permute-start | bytes 1769480 | tf_op jit(solution)/shard_map/ppermute | solution.py:642
  152.2 25.7 %collective-permute-start.6 = (bf16[384,768]{1,0:T(8,128)(2,1)S(1)}, bf16[384,768]{1,0:T(8,128)(2,1)}, u32[]{:S(2)}, u32[]{:S(2)}) collective-permute-start(bf16[384,768]{1,0:T(8,128)(2,1)S(1)} %collective-permute-done.3), channel_id=1, source_target_pairs={{0,1},{1,0},{2,3},{3,2},{4,5},{5,4},{6,7},{7,6},{8,9},{9,8},{10,11... | collective-permute-start | bytes 1769480 | tf_op jit(solution)/shard_map/ppermute | solution.py:642
  154.4 23.4 %collective-permute-start.36 = (bf16[384,768]{1,0:T(8,128)(2,1)S(1)}, bf16[384,768]{1,0:T(8,128)(2,1)S(1)}, u32[]{:S(2)}, u32[]{:S(2)}) collective-permute-start(bf16[384,768]{1,0:T(8,128)(2,1)S(1)} %collective-permute-done.33), channel_id=1, source_target_pairs={{0,1},{1,0},{2,3},{3,2},{4,5},{5,4},{6,7},{7,6},{8,9},{9,8},{10,11... | collective-permute-start | bytes 1769480 | tf_op jit(solution)/shard_map/ppermute | solution.py:642
  155.6 107.2 %collective-permute-start.30 = (bf16[96,3072]{1,0:T(8,128)(2,1)}, bf16[96,3072]{1,0:T(8,128)(2,1)}, u32[]{:S(2)}, u32[]{:S(2)}) collective-permute-start(bf16[96,3072]{1,0:T(8,128)(2,1)} %collective-permute-done.27), channel_id=1, source_target_pairs={{0,1},{1,0},{2,3},{3,2},{4,5},{5,4},{6,7},{7,6},{8,9},{9,8},{10,11... | collective-permute-start | bytes 1769480 | tf_op jit(solution)/shard_map/ppermute | solution.py:642
  240.0 27.1 %collective-permute-start.16 = (bf16[384,192]{1,0:T(8,128)(2,1)S(1)}, bf16[384,192]{1,0:T(8,128)(2,1)S(1)}, u32[]{:S(2)}, u32[]{:S(2)}) collective-permute-start(bf16[384,192]{1,0:T(8,128)(2,1)S(1)} %get-tuple-element.80), channel_id=1, source_target_pairs={{0,2},{1,3},{2,0},{3,1},{4,6},{5,7},{6,4},{7,5},{8,10},{9,11},{10,... | collective-permute-start | bytes 442376 | tf_op jit(solution)/shard_map/ppermute | solution.py:642
  252.4 14.7 %collective-permute-start.17 = (bf16[384,192]{1,0:T(8,128)(2,1)S(1)}, bf16[384,192]{1,0:T(8,128)(2,1)S(1)}, u32[]{:S(2)}, u32[]{:S(2)}) collective-permute-start(bf16[384,192]{1,0:T(8,128)(2,1)S(1)} %get-tuple-element.79), channel_id=1, source_target_pairs={{0,4},{1,5},{2,6},{3,7},{4,0},{5,1},{6,2},{7,3},{8,12},{9,13},{10,... | collective-permute-start | bytes 442376 | tf_op jit(solution)/shard_map/ppermute | solution.py:642
  253.6 13.5 %collective-permute-start.18 = (bf16[384,192]{1,0:T(8,128)(2,1)S(1)}, bf16[384,192]{1,0:T(8,128)(2,1)S(1)}, u32[]{:S(2)}, u32[]{:S(2)}) collective-permute-start(bf16[384,192]{1,0:T(8,128)(2,1)S(1)} %get-tuple-element.78), channel_id=1, source_target_pairs={{0,6},{1,7},{2,4},{3,5},{4,2},{5,3},{6,0},{7,1},{8,14},{9,15},{10,... | collective-permute-start | bytes 442376 | tf_op jit(solution)/shard_map/ppermute | solution.py:642
  291.6 69.8 %collective-permute-start.55 = (bf16[384,768]{0,1:T(8,128)(2,1)}, bf16[384,768]{0,1:T(8,128)(2,1)}, u32[]{:S(2)}, u32[]{:S(2)}) collective-permute-start(bf16[384,768]{0,1:T(8,128)(2,1)} %bitcast.41), channel_id=1, source_target_pairs={{0,1},{1,0},{2,3},{3,2},{4,5},{5,4},{6,7},{7,6},{8,9},{9,8},{10,11... | collective-permute-start | bytes 1769480 | tf_op jit(solution)/shard_map/ppermute | solution.py:642
  302.6 132.5 %collective-permute-start.67 = (bf16[384,768]{1,0:T(8,128)(2,1)}, bf16[384,768]{1,0:T(8,128)(2,1)}, u32[]{:S(2)}, u32[]{:S(2)}) collective-permute-start(bf16[384,768]{1,0:T(8,128)(2,1)} %copy-done.13), channel_id=1, source_target_pairs={{0,1},{1,0},{2,3},{3,2},{4,5},{5,4},{6,7},{7,6},{8,9},{9,8},{10,11... | collective-permute-start | bytes 1769480 | tf_op jit(solution)/shard_map/ppermute | solution.py:642
  308.5 56.0 %collective-permute-start.37 = (bf16[384,192]{1,0:T(8,128)(2,1)}, bf16[384,192]{1,0:T(8,128)(2,1)}, u32[]{:S(2)}, u32[]{:S(2)}) collective-permute-start(bf16[384,192]{1,0:T(8,128)(2,1)} %bitcast.442), channel_id=1, source_target_pairs={{0,2},{1,3},{2,0},{3,1},{4,6},{5,7},{6,4},{7,5},{8,10},{9,11},{10,... | collective-permute-start | bytes 442376 | tf_op jit(solution)/shard_map/ppermute | solution.py:642
  313.3 46.6 %collective-permute-start.56 = (bf16[384,384]{1,0:T(8,128)(2,1)}, bf16[384,384]{1,0:T(8,128)(2,1)}, u32[]{:S(2)}, u32[]{:S(2)}) collective-permute-start(bf16[384,384]{1,0:T(8,128)(2,1)} %bitcast.387), channel_id=1, source_target_pairs={{0,1},{1,0},{2,3},{3,2},{4,5},{5,4},{6,7},{7,6},{8,9},{9,8},{10,11... | collective-permute-start | bytes 884744 | tf_op jit(solution)/shard_map/ppermute | solution.py:642
  359.9 16.8 %collective-permute-start.38 = (bf16[384,192]{1,0:T(8,128)(2,1)}, bf16[384,192]{1,0:T(8,128)(2,1)S(1)}, u32[]{:S(2)}, u32[]{:S(2)}) collective-permute-start(bf16[384,192]{1,0:T(8,128)(2,1)} %bitcast.72), channel_id=1, source_target_pairs={{0,4},{1,5},{2,6},{3,7},{4,0},{5,1},{6,2},{7,3},{8,12},{9,13},{10,... | collective-permute-start | bytes 442376 | tf_op jit(solution)/shard_map/ppermute | solution.py:642
  361.4 23.2 %collective-permute-start.39 = (bf16[384,192]{1,0:T(8,128)(2,1)}, bf16[384,192]{1,0:T(8,128)(2,1)S(1)}, u32[]{:S(2)}, u32[]{:S(2)}) collective-permute-start(bf16[384,192]{1,0:T(8,128)(2,1)} %bitcast.74), channel_id=1, source_target_pairs={{0,6},{1,7},{2,4},{3,5},{4,2},{5,3},{6,0},{7,1},{8,14},{9,15},{10,... | collective-permute-start | bytes 442376 | tf_op jit(solution)/shard_map/ppermute | solution.py:642
  370.3 8.6 %collective-permute-start.57 = (bf16[256,384]{1,0:T(8,128)(2,1)S(1)}, bf16[256,384]{1,0:T(8,128)(2,1)S(1)}, u32[]{:S(2)}, u32[]{:S(2)}) collective-permute-start(bf16[256,384]{1,0:T(8,128)(2,1)S(1)} %get-tuple-element.70), channel_id=1, source_target_pairs={{0,8},{1,17},{2,10},{3,19},{4,12},{5,21},{6,14},{7,23},{8,0},{9,25... | collective-permute-start | bytes 589832 | tf_op jit(solution)/shard_map/ppermute | solution.py:642
  388.8 46.5 %collective-permute-start.68 = (bf16[384,1536]{1,0:T(8,128)(2,1)S(1)}, bf16[384,1536]{1,0:T(8,128)(2,1)}, u32[]{:S(2)}, u32[]{:S(2)}) collective-permute-start(bf16[384,1536]{1,0:T(8,128)(2,1)S(1)} %bitcast.430), channel_id=1, source_target_pairs={{0,1},{1,0},{2,3},{3,2},{4,5},{5,4},{6,7},{7,6},{8,9},{9,8},{10,11... | collective-permute-start | bytes 3538952 | tf_op jit(solution)/shard_map/ppermute | solution.py:642
  390.0 51.8 %collective-permute-start.79 = (bf16[384,1536]{0,1:T(8,128)(2,1)S(1)}, bf16[384,1536]{0,1:T(8,128)(2,1)}, u32[]{:S(2)}, u32[]{:S(2)}) collective-permute-start(bf16[384,1536]{0,1:T(8,128)(2,1)S(1)} %bitcast.429), channel_id=1, source_target_pairs={{0,1},{1,0},{2,3},{3,2},{4,5},{5,4},{6,7},{7,6},{8,9},{9,8},{10,11... | collective-permute-start | bytes 3538952 | tf_op jit(solution)/shard_map/ppermute | solution.py:642
  390.0 31.7 %collective-permute-start.63 = (bf16[64,384]{1,0:T(8,128)(2,1)S(1)}, bf16[64,384]{1,0:T(8,128)(2,1)S(1)}, u32[]{:S(2)}, u32[]{:S(2)}) collective-permute-start(bf16[64,384]{1,0:T(8,128)(2,1)S(1)} %get-tuple-element.48), channel_id=1, source_target_pairs={{0,2},{1,3},{2,0},{3,1},{4,6},{5,7},{6,4},{7,5},{8,10},{9,11},{10,... | collective-permute-start | bytes 147464 | tf_op jit(solution)/shard_map/ppermute | solution.py:642
  433.2 18.4 %collective-permute-start.40 = (bf16[4,384,384]{2,1,0:T(8,128)(2,1)}, bf16[4,384,384]{2,1,0:T(8,128)(2,1)}, u32[]{:S(2)}, u32[]{:S(2)}) collective-permute-start(bf16[4,384,384]{2,1,0:T(8,128)(2,1)} %get-tuple-element.26), channel_id=1, source_target_pairs={{0,1},{1,0},{2,3},{3,2},{4,5},{5,4},{6,7},{7,6},{8,9},{9,8},{10,11... | collective-permute-start | bytes 3538952 | tf_op jit(solution)/shard_map/ppermute | solution.py:642
  435.2 14.2 %collective-permute-start.66 = (bf16[256,384]{1,0:T(8,128)(2,1)S(1)}, bf16[256,384]{1,0:T(8,128)(2,1)S(1)}, u32[]{:S(2)}, u32[]{:S(2)}) collective-permute-start(bf16[256,384]{1,0:T(8,128)(2,1)S(1)} %bitcast.432), channel_id=1, source_target_pairs={{0,1},{1,0},{2,3},{3,2},{4,5},{5,4},{6,7},{7,6},{8,9},{9,8},{10,11... | collective-permute-start | bytes 589832 | tf_op jit(solution)/shard_map/ppermute | solution.py:642
  439.7 35.9 %collective-permute-start.70 = (bf16[192,1536]{1,0:T(8,128)(2,1)}, bf16[192,1536]{1,0:T(8,128)(2,1)}, u32[]{:S(2)}, u32[]{:S(2)}) collective-permute-start(bf16[192,1536]{1,0:T(8,128)(2,1)} %get-tuple-element.61), channel_id=1, source_target_pairs={{0,8},{1,17},{2,10},{3,19},{4,12},{5,21},{6,14},{7,23},{8,0},{9,25... | collective-permute-start | bytes 1769480 | tf_op jit(solution)/shard_map/ppermute | solution.py:642
  441.3 112.0 %collective-permute-start.69 = (bf16[192,1536]{1,0:T(8,128)(2,1)}, bf16[192,1536]{1,0:T(8,128)(2,1)}, u32[]{:S(2)}, u32[]{:S(2)}) collective-permute-start(bf16[192,1536]{1,0:T(8,128)(2,1)} %get-tuple-element.60), channel_id=1, source_target_pairs={{0,8},{1,17},{2,10},{3,19},{4,12},{5,21},{6,14},{7,23},{8,0},{9,25... | collective-permute-start | bytes 1769480 | tf_op jit(solution)/shard_map/ppermute | solution.py:642
  447.9 30.4 %collective-permute-start.82 = (bf16[384,768]{1,0:T(8,128)(2,1)}, bf16[384,768]{1,0:T(8,128)(2,1)}, u32[]{:S(2)}, u32[]{:S(2)}) collective-permute-start(bf16[384,768]{1,0:T(8,128)(2,1)} %get-tuple-element.59), channel_id=1, source_target_pairs={{0,8},{1,17},{2,10},{3,19},{4,12},{5,21},{6,14},{7,23},{8,0},{9,25... | collective-permute-start | bytes 1769480 | tf_op jit(solution)/shard_map/ppermute | solution.py:642
  468.5 16.3 %collective-permute-start.43 = (bf16[384,576]{1,0:T(8,128)(2,1)}, bf16[384,576]{1,0:T(8,128)(2,1)}, u32[]{:S(2)}, u32[]{:S(2)}) collective-permute-start(bf16[384,576]{1,0:T(8,128)(2,1)} %get-tuple-element.69), channel_id=1, source_target_pairs={{0,6},{1,7},{2,4},{3,5},{4,2},{5,3},{6,0},{7,1},{8,14},{9,15},{10,... | collective-permute-start | bytes 1327112 | tf_op jit(solution)/shard_map/ppermute | solution.py:642
  470.5 42.2 %collective-permute-start.42 = (bf16[384,576]{1,0:T(8,128)(2,1)}, bf16[384,576]{1,0:T(8,128)(2,1)}, u32[]{:S(2)}, u32[]{:S(2)}) collective-permute-start(bf16[384,576]{1,0:T(8,128)(2,1)} %get-tuple-element.68), channel_id=1, source_target_pairs={{0,4},{1,5},{2,6},{3,7},{4,0},{5,1},{6,2},{7,3},{8,12},{9,13},{10,... | collective-permute-start | bytes 1327112 | tf_op jit(solution)/shard_map/ppermute | solution.py:642
  478.3 23.9 %collective-permute-start.41 = (bf16[384,576]{1,0:T(8,128)(2,1)S(1)}, bf16[384,576]{1,0:T(8,128)(2,1)S(1)}, u32[]{:S(2)}, u32[]{:S(2)}) collective-permute-start(bf16[384,576]{1,0:T(8,128)(2,1)S(1)} %copy-done.29), channel_id=1, source_target_pairs={{0,2},{1,3},{2,0},{3,1},{4,6},{5,7},{6,4},{7,5},{8,10},{9,11},{10,... | collective-permute-start | bytes 1327112 | tf_op jit(solution)/shard_map/ppermute | solution.py:642
  483.2 31.6 %collective-permute-start.46 = (bf16[112,576]{1,0:T(8,128)(2,1)S(1)}, bf16[112,576]{1,0:T(8,128)(2,1)S(1)}, u32[]{:S(2)}, u32[]{:S(2)}) collective-permute-start(bf16[112,576]{1,0:T(8,128)(2,1)S(1)} %get-tuple-element.77), channel_id=1, source_target_pairs={{0,8},{1,17},{2,10},{3,19},{4,12},{5,21},{6,14},{7,23},{8,0},{9,25... | collective-permute-start | bytes 387080 | tf_op jit(solution)/shard_map/ppermute | solution.py:642
  484.8 30.7 %collective-permute-start.45 = (bf16[112,576]{1,0:T(8,128)(2,1)S(1)}, bf16[112,576]{1,0:T(8,128)(2,1)S(1)}, u32[]{:S(2)}, u32[]{:S(2)}) collective-permute-start(bf16[112,576]{1,0:T(8,128)(2,1)S(1)} %get-tuple-element.76), channel_id=1, source_target_pairs={{0,8},{1,17},{2,10},{3,19},{4,12},{5,21},{6,14},{7,23},{8,0},{9,25... | collective-permute-start | bytes 387080 | tf_op jit(solution)/shard_map/ppermute | solution.py:642
  521.6 12.9 %collective-permute-start.49 = (bf16[112,576]{1,0:T(8,128)(2,1)S(1)}, bf16[112,576]{1,0:T(8,128)(2,1)S(1)}, u32[]{:S(2)}, u32[]{:S(2)}) collective-permute-start(bf16[112,576]{1,0:T(8,128)(2,1)S(1)} %fusion.81), channel_id=1, source_target_pairs={{0,4},{1,5},{2,6},{3,7},{4,0},{5,1},{6,2},{7,3},{8,12},{9,13},{10,... | collective-permute-start | bytes 387080 | tf_op jit(solution)/shard_map/ppermute | solution.py:642
  524.1 10.5 %collective-permute-start.50 = (bf16[112,576]{1,0:T(8,128)(2,1)S(1)}, bf16[112,576]{1,0:T(8,128)(2,1)S(1)}, u32[]{:S(2)}, u32[]{:S(2)}) collective-permute-start(bf16[112,576]{1,0:T(8,128)(2,1)S(1)} %fusion.81), channel_id=1, source_target_pairs={{0,6},{1,7},{2,4},{3,5},{4,2},{5,3},{6,0},{7,1},{8,14},{9,15},{10,... | collective-permute-start | bytes 387080 | tf_op jit(solution)/shard_map/ppermute | solution.py:642
  525.9 9.5 %collective-permute-start.51 = (bf16[112,576]{1,0:T(8,128)(2,1)S(1)}, bf16[112,576]{1,0:T(8,128)(2,1)S(1)}, u32[]{:S(2)}, u32[]{:S(2)}) collective-permute-start(bf16[112,576]{1,0:T(8,128)(2,1)S(1)} %fusion.81), channel_id=1, source_target_pairs={{0,1},{1,0},{2,3},{3,2},{4,5},{5,4},{6,7},{7,6},{8,9},{9,8},{10,11... | collective-permute-start | bytes 387080 | tf_op jit(solution)/shard_map/ppermute | solution.py:642
  535.4 24.2 %collective-permute-start.81 = (bf16[384,768]{1,0:T(8,128)(2,1)}, bf16[384,768]{1,0:T(8,128)(2,1)S(1)}, u32[]{:S(2)}, u32[]{:S(2)}) collective-permute-start(bf16[384,768]{1,0:T(8,128)(2,1)} %get-tuple-element.58), channel_id=1, source_target_pairs={{0,8},{1,17},{2,10},{3,19},{4,12},{5,21},{6,14},{7,23},{8,0},{9,25... | collective-permute-start | bytes 1769480 | tf_op jit(solution)/shard_map/ppermute | solution.py:642
  537.3 15.9 %collective-permute-start.71 = (bf16[192,1536]{1,0:T(8,128)(2,1)}, bf16[192,1536]{1,0:T(8,128)(2,1)}, u32[]{:S(2)}, u32[]{:S(2)}) collective-permute-start(bf16[192,1536]{1,0:T(8,128)(2,1)} %fusion.36), channel_id=1, source_target_pairs={{0,16},{1,9},{2,18},{3,11},{4,20},{5,13},{6,22},{7,15},{8,24},{9,1... | collective-permute-start | bytes 1769480 | tf_op jit(solution)/shard_map/ppermute | solution.py:642
  537.5 22.1 %collective-permute-start.83 = (bf16[384,768]{1,0:T(8,128)(2,1)}, bf16[384,768]{1,0:T(8,128)(2,1)}, u32[]{:S(2)}, u32[]{:S(2)}) collective-permute-start(bf16[384,768]{1,0:T(8,128)(2,1)} %fusion.34), channel_id=1, source_target_pairs={{0,16},{1,9},{2,18},{3,11},{4,20},{5,13},{6,22},{7,15},{8,24},{9,1... | collective-permute-start | bytes 1769480 | tf_op jit(solution)/shard_map/ppermute | solution.py:642
  555.2 8.9 %collective-permute-start.74 = (bf16[48,1536]{1,0:T(8,128)(2,1)S(1)}, bf16[48,1536]{1,0:T(8,128)(2,1)S(1)}, u32[]{:S(2)}, u32[]{:S(2)}) collective-permute-start(bf16[48,1536]{1,0:T(8,128)(2,1)S(1)} %get-tuple-element.87), channel_id=1, source_target_pairs={{0,6},{1,7},{2,4},{3,5},{4,2},{5,3},{6,0},{7,1},{8,14},{9,15},{10,... | collective-permute-start | bytes 442376 | tf_op jit(solution)/shard_map/ppermute | solution.py:642
  557.3 20.0 %collective-permute-start.73 = (bf16[48,1536]{1,0:T(8,128)(2,1)S(1)}, bf16[48,1536]{1,0:T(8,128)(2,1)S(1)}, u32[]{:S(2)}, u32[]{:S(2)}) collective-permute-start(bf16[48,1536]{1,0:T(8,128)(2,1)S(1)} %get-tuple-element.88), channel_id=1, source_target_pairs={{0,4},{1,5},{2,6},{3,7},{4,0},{5,1},{6,2},{7,3},{8,12},{9,13},{10,... | collective-permute-start | bytes 442376 | tf_op jit(solution)/shard_map/ppermute | solution.py:642
  558.8 18.6 %collective-permute-start.72 = (bf16[48,1536]{1,0:T(8,128)(2,1)S(1)}, bf16[48,1536]{1,0:T(8,128)(2,1)S(1)}, u32[]{:S(2)}, u32[]{:S(2)}) collective-permute-start(bf16[48,1536]{1,0:T(8,128)(2,1)S(1)} %get-tuple-element.86), channel_id=1, source_target_pairs={{0,2},{1,3},{2,0},{3,1},{4,6},{5,7},{6,4},{7,5},{8,10},{9,11},{10,... | collective-permute-start | bytes 442376 | tf_op jit(solution)/shard_map/ppermute | solution.py:642
  561.3 18.8 %collective-permute-start.86 = (bf16[96,768]{1,0:T(8,128)(2,1)S(1)}, bf16[96,768]{1,0:T(8,128)(2,1)S(1)}, u32[]{:S(2)}, u32[]{:S(2)}) collective-permute-start(bf16[96,768]{1,0:T(8,128)(2,1)S(1)} %get-tuple-element.84), channel_id=1, source_target_pairs={{0,6},{1,7},{2,4},{3,5},{4,2},{5,3},{6,0},{7,1},{8,14},{9,15},{10,... | collective-permute-start | bytes 442376 | tf_op jit(solution)/shard_map/ppermute | solution.py:642
  563.4 26.6 %collective-permute-start.85 = (bf16[96,768]{1,0:T(8,128)(2,1)S(1)}, bf16[96,768]{1,0:T(8,128)(2,1)S(1)}, u32[]{:S(2)}, u32[]{:S(2)}) collective-permute-start(bf16[96,768]{1,0:T(8,128)(2,1)S(1)} %get-tuple-element.85), channel_id=1, source_target_pairs={{0,4},{1,5},{2,6},{3,7},{4,0},{5,1},{6,2},{7,3},{8,12},{9,13},{10,... | collective-permute-start | bytes 442376 | tf_op jit(solution)/shard_map/ppermute | solution.py:642
  564.0 26.0 %collective-permute-start.84 = (bf16[96,768]{1,0:T(8,128)(2,1)S(1)}, bf16[96,768]{1,0:T(8,128)(2,1)S(1)}, u32[]{:S(2)}, u32[]{:S(2)}) collective-permute-start(bf16[96,768]{1,0:T(8,128)(2,1)S(1)} %get-tuple-element.83), channel_id=1, source_target_pairs={{0,2},{1,3},{2,0},{3,1},{4,6},{5,7},{6,4},{7,5},{8,10},{9,11},{10,... | collective-permute-start | bytes 442376 | tf_op jit(solution)/shard_map/ppermute | solution.py:642
  577.5 15.3 %collective-permute-start.75 = (bf16[48,1536]{1,0:T(8,128)(2,1)S(1)}, bf16[48,1536]{1,0:T(8,128)(2,1)S(1)}, u32[]{:S(2)}, u32[]{:S(2)}) collective-permute-start(bf16[48,1536]{1,0:T(8,128)(2,1)S(1)} %get-tuple-element.44), channel_id=1, source_target_pairs={{0,2},{1,3},{2,0},{3,1},{4,6},{5,7},{6,4},{7,5},{8,10},{9,11},{10,... | collective-permute-start | bytes 442376 | tf_op jit(solution)/shard_map/ppermute | solution.py:642
  577.5 17.1 %collective-permute-start.76 = (bf16[48,1536]{1,0:T(8,128)(2,1)S(1)}, bf16[48,1536]{1,0:T(8,128)(2,1)S(1)}, u32[]{:S(2)}, u32[]{:S(2)}) collective-permute-start(bf16[48,1536]{1,0:T(8,128)(2,1)S(1)} %get-tuple-element.44), channel_id=1, source_target_pairs={{0,4},{1,5},{2,6},{3,7},{4,0},{5,1},{6,2},{7,3},{8,12},{9,13},{10,... | collective-permute-start | bytes 442376 | tf_op jit(solution)/shard_map/ppermute | solution.py:642
  580.1 14.6 %collective-permute-start.77 = (bf16[48,1536]{1,0:T(8,128)(2,1)S(1)}, bf16[48,1536]{1,0:T(8,128)(2,1)S(1)}, u32[]{:S(2)}, u32[]{:S(2)}) collective-permute-start(bf16[48,1536]{1,0:T(8,128)(2,1)S(1)} %get-tuple-element.44), channel_id=1, source_target_pairs={{0,6},{1,7},{2,4},{3,5},{4,2},{5,3},{6,0},{7,1},{8,14},{9,15},{10,... | collective-permute-start | bytes 442376 | tf_op jit(solution)/shard_map/ppermute | solution.py:642
  590.3 15.6 %collective-permute-start.88 = (bf16[96,768]{1,0:T(8,128)(2,1)S(1)}, bf16[96,768]{1,0:T(8,128)(2,1)S(1)}, u32[]{:S(2)}, u32[]{:S(2)}) collective-permute-start(bf16[96,768]{1,0:T(8,128)(2,1)S(1)} %get-tuple-element.40), channel_id=1, source_target_pairs={{0,4},{1,5},{2,6},{3,7},{4,0},{5,1},{6,2},{7,3},{8,12},{9,13},{10,... | collective-permute-start | bytes 442376 | tf_op jit(solution)/shard_map/ppermute | solution.py:642
  592.8 13.1 %collective-permute-start.89 = (bf16[96,768]{1,0:T(8,128)(2,1)S(1)}, bf16[96,768]{1,0:T(8,128)(2,1)S(1)}, u32[]{:S(2)}, u32[]{:S(2)}) collective-permute-start(bf16[96,768]{1,0:T(8,128)(2,1)S(1)} %get-tuple-element.40), channel_id=1, source_target_pairs={{0,6},{1,7},{2,4},{3,5},{4,2},{5,3},{6,0},{7,1},{8,14},{9,15},{10,... | collective-permute-start | bytes 442376 | tf_op jit(solution)/shard_map/ppermute | solution.py:642
  594.7 11.3 %collective-permute-start.78 = (bf16[192,1536]{1,0:T(8,128)(2,1)S(1)}, bf16[192,1536]{1,0:T(8,128)(2,1)S(1)}, u32[]{:S(2)}, u32[]{:S(2)}) collective-permute-start(bf16[192,1536]{1,0:T(8,128)(2,1)S(1)} %bitcast.421), channel_id=1, source_target_pairs={{0,1},{1,0},{2,3},{3,2},{4,5},{5,4},{6,7},{7,6},{8,9},{9,8},{10,11... | collective-permute-start | bytes 1769480 | tf_op jit(solution)/shard_map/ppermute | solution.py:642
  (81 other events, 609.0 us)
